TPU v7x, 32 devices: a whole 2x2x4 slice. The times are simulated.
32 devices in a mesh: date: 4 (over z), az: 8 (over y, x, core).
Axes of the slice: x: 2, y: 2, z: 4, core: 2. Of those that a mesh axis runs over, the one named last changes fastest.
Arguments:
- slc_stack: bfloat16 [2, 256, 256, 128], P(None, 'date', 'az'), may hold values from -6 to 6
- fir_taps: float32 [256, 5], P('date'), may hold values from 0.1 to 1
- look_index: int32 [8, 4, 64], P('az', 'date'), may hold values from 0 to 1023
- shrink_level: int32 [8, 4], P('az', 'date'), may hold values from 1 to 12
- window_half: int32 [256], replicated, may hold values from 0 to 2
- basis: bfloat16 [32, 256], replicated, may hold values from -0.375 to 0.375
Outputs:
- projection: float32 [32, 2, 256, 128], P('date', None, 'az')
Inputs may be any that keep to these rules, and one draw needn't show every extreme that they name: `look_index`: pixel numbers inside one block of 8 rows.
All inputs are finite; a program needn't handle non-finite values.
Results may differ from a plain program's by a relative error of at most 0.0048.
Values may be sent and summed in bfloat16 or wider, within the bound.
A program may use at most 64 MiB of HBM per device.

v0:
```python
import jax
import jax.numpy as jnp
from jax import lax
from jax.sharding import PartitionSpec as P

NS_ITERS = 6
SMOOTH_REACH = 2


def padded_2(block, sides, width, periodic):
    for axis, dim in sides:
        count = lax.axis_size(axis)
        forward = [(i, i + 1) for i in range(count - 1)]
        if periodic:
            forward.append((count - 1, 0))
        backward = [(target, source) for source, target in forward]
        low = lax.ppermute(
            lax.slice_in_dim(block, block.shape[dim] - width, None, axis=dim), axis, forward
        )
        high = lax.ppermute(lax.slice_in_dim(block, 0, width, axis=dim), axis, backward)
        block = jnp.concatenate([low, block, high], axis=dim)
    return block


def shifted(shard, axis, by):
    length = lax.axis_size(axis)
    pairs = [(i, i + by) for i in range(length) if 0 <= i + by < length]
    return lax.ppermute(shard, axis, pairs)


def complex_product(left_re, left_im, right_re, right_im):
    highest = lax.Precision.HIGHEST
    real = jnp.dot(left_re, right_re, precision=highest) - jnp.dot(
        left_im, right_im, precision=highest
    )
    imag = jnp.dot(left_re, right_im, precision=highest) + jnp.dot(
        left_im, right_re, precision=highest
    )
    return (real, imag)


def wiener_block(pixels, chosen, level):
    sample = jnp.take(pixels, chosen, axis=2)
    samp_re = sample[0]
    samp_im = sample[1]
    looks = chosen.shape[0]
    gram_re = (
        jnp.dot(samp_re, samp_re.T, preferred_element_type=jnp.float32)
        + jnp.dot(samp_im, samp_im.T, preferred_element_type=jnp.float32)
    ) / looks
    gram_im = (
        jnp.dot(samp_im, samp_re.T, preferred_element_type=jnp.float32)
        - jnp.dot(samp_re, samp_im.T, preferred_element_type=jnp.float32)
    ) / looks
    count = gram_re.shape[0]
    identity = jnp.eye(count, dtype=jnp.float32)
    level_mean = jnp.trace(gram_re) / count + 1e-06
    weight = level.astype(jnp.float32) / 16.0
    shrunk_re = (1.0 - weight) * gram_re + weight * level_mean * identity
    shrunk_im = (1.0 - weight) * gram_im
    load_re = shrunk_re + level_mean * identity
    scale = 1.0 / jnp.sqrt(jnp.sum(load_re * load_re + shrunk_im * shrunk_im))
    inv_re = identity * scale
    inv_im = jnp.zeros_like(identity)
    for step in range(NS_ITERS):
        prod_re, prod_im = complex_product(load_re, shrunk_im, inv_re, inv_im)
        inv_re, inv_im = complex_product(inv_re, inv_im, 2.0 * identity - prod_re, -prod_im)
    gain_re, gain_im = complex_product(shrunk_re, shrunk_im, inv_re, inv_im)
    gain_re = gain_re.astype(jnp.bfloat16)
    gain_im = gain_im.astype(jnp.bfloat16)
    pix_re = pixels[0]
    pix_im = pixels[1]
    out_re = jnp.dot(gain_re, pix_re, preferred_element_type=jnp.float32) - jnp.dot(
        gain_im, pix_im, preferred_element_type=jnp.float32
    )
    out_im = jnp.dot(gain_re, pix_im, preferred_element_type=jnp.float32) + jnp.dot(
        gain_im, pix_re, preferred_element_type=jnp.float32
    )
    return jnp.stack([out_re, out_im]).astype(jnp.bfloat16)


def smooth_weights(halves, reach):
    offsets = jnp.arange(-reach, reach + 1)
    inside = (jnp.abs(offsets)[None, :] <= halves[:, None]).astype(jnp.float32)
    return inside / (2 * halves + 1).astype(jnp.float32)[:, None]


def smooth_rows(rim, weights, length):
    smoothed = jnp.zeros((rim.shape[0], rim.shape[1], length, rim.shape[3]), jnp.float32)
    for offset in range(2 * SMOOTH_REACH + 1):
        smoothed = smoothed + weights[:, offset][:, None, None] * rim[
            :, :, offset : offset + length, :
        ].astype(jnp.float32)
    return smoothed.astype(jnp.bfloat16)


def on_device(slc_stack, fir_taps, look_index, shrink_level, window_half, basis):
    date_local = slc_stack.shape[1]
    rows = slc_stack.shape[2]
    columns = slc_stack.shape[3]
    groups = lax.axis_size("date")
    block_pixels = rows * columns // groups
    block_rows = rows // groups
    reach = (fir_taps.shape[1] - 1) // 2
    padded = padded_2(slc_stack, (("az", 2),), reach, False)
    filtered = jnp.zeros(slc_stack.shape, jnp.float32)
    for offset in range(2 * reach + 1):
        filtered = filtered + fir_taps[:, offset][:, None, None] * padded[
            :, :, offset : offset + rows, :
        ].astype(jnp.float32)
    filtered = filtered.astype(jnp.bfloat16)
    grouped = filtered.reshape(2, date_local, groups, block_pixels)
    stacked = lax.all_to_all(grouped, "date", split_axis=2, concat_axis=1, tiled=True)
    wiener = wiener_block(stacked[:, :, 0, :], look_index[0, 0], shrink_level[0, 0])
    bases = basis.shape[0]
    own_bases = bases // groups
    all_dates = wiener.shape[1]
    block_now = wiener.reshape(2, all_dates, block_rows, columns)
    extended = padded_2(block_now, (("date", 2),), SMOOTH_REACH, True)
    above = extended[:, :, :SMOOTH_REACH, :]
    below = extended[:, :, block_rows + SMOOTH_REACH :, :]
    above_far = shifted(above, "az", 1)
    below_far = shifted(below, "az", -1)
    position = lax.axis_index("date")
    above = jnp.where(position == 0, above_far, above)
    below = jnp.where(position == groups - 1, below_far, below)
    rim = jnp.concatenate([above, block_now, below], axis=2)
    smoothed = smooth_rows(rim, smooth_weights(window_half, SMOOTH_REACH), block_rows)
    whole = jnp.einsum(
        "kt,ctp->kcp",
        basis,
        smoothed.reshape(2, all_dates, block_pixels),
        preferred_element_type=jnp.float32,
    )
    homed = lax.all_to_all(whole[:, :, None, :], "date", split_axis=0, concat_axis=2, tiled=True)
    projection = homed.reshape(own_bases, 2, rows, columns)
    return projection


def solution(mesh):
    in_specs = (
        P(None, "date", "az", None),
        P("date", None),
        P("az", "date", None),
        P("az", "date"),
        P(),
        P(),
    )
    out_specs = P("date", None, "az", None)
    return jax.shard_map(
        on_device, mesh=mesh, in_specs=in_specs, out_specs=out_specs, check_vma=False
    )
```

profile of v0, /device:TPU:3, one launch (start us, length us, event | category | flops | bytes accessed | tf_op | source)
XLA Modules:
  0.0 109.8 jit_solution(7447028840527217587)
XLA Ops:
  0.0 1.2 %fusion.83 = (bf16[2,64,2,128]{3,2,1,0:T(2,128)(2,1)S(1)}, bf16[2,64,2,128]{3,2,1,0:T(2,128)(2,1)S(1)}) fusion(bf16[2,64,32,128]{3,2,1,0:T(8,128)(2,1)} %param.6), kind=kLoop, calls=%fused_computation.153 | loop fusion | bytes 262144 | tf_op jit(solution)/shard_map/slice | solution.py:20
  1.2 2.6 %collective-permute-start.1 = (bf16[2,64,2,128]{3,2,1,0:T(2,128)(2,1)S(1)}, bf16[2,64,2,128]{3,2,1,0:T(2,128)(2,1)S(1)}, u32[]{:S(2)}, u32[]{:S(2)}) collective-permute-start(bf16[2,64,2,128]{3,2,1,0:T(2,128)(2,1)S(1)} %get-tuple-element.11), channel_id=1, source_target_pairs={{1,0},{2,1},{3,2},{4,3},{5,4},{6,5},{7,6},{9,8},{10,9},{11,10},{12... | collective-permute-start | bytes 196616 | tf_op jit(solution)/shard_map/ppermute | solution.py:20
  3.8 3.9 %collective-permute-start = (bf16[2,64,2,128]{3,2,1,0:T(2,128)(2,1)S(1)}, bf16[2,64,2,128]{3,2,1,0:T(2,128)(2,1)S(1)}, u32[]{:S(2)}, u32[]{:S(2)}) collective-permute-start(bf16[2,64,2,128]{3,2,1,0:T(2,128)(2,1)S(1)} %get-tuple-element.12), channel_id=1, source_target_pairs={{0,1},{1,2},{2,3},{3,4},{4,5},{5,6},{6,7},{8,9},{9,10},{10,11},{11... | collective-permute-start | bytes 196616 | tf_op jit(solution)/shard_map/ppermute | solution.py:17
  7.7 0.9 slice_bitcast_fusion.4
  8.6 1.3 %constant_dynamic-update-slice_fusion.1 = bf16[2,64,34,128]{3,2,1,0:T(8,128)(2,1)S(1)} fusion(bf16[2,64,32,128]{3,2,1,0:T(8,128)(2,1)} %param.6), kind=kLoop, calls=%fused_computation.112 | loop fusion | bytes 2097152
  10.0 1.8 %add_convert_fusion.1 = bf16[2,64,32,128]{3,2,1,0:T(8,128)(2,1)S(1)} fusion(bf16[2,64,32,128]{3,2,1,0:T(8,128)(2,1)S(1)} %copy-done.1, bf16[2,64,2,128]{3,2,1,0:T(2,128)(2,1)S(1)} %collective-permute-done, bf16[2,64,34,128]{3,2,1,0:T(8,128)(2,1)S(1)} %constant_dynamic-update-slice_fusion, f32[64]{0:T(128)S(1)} %get-tuple-element.23, ...), kind=kLoop, calls=%fused_computation.6 | loop fusion | flops 11010048 | bytes 4261120 | tf_op jit(solution)/shard_map/convert_element_type | solution.py:111
  12.1 1.3 %copy.15 = bf16[2,64,4,1024]{3,1,0,2:T(8,128)(2,1)} copy(bf16[2,64,4,1024]{3,2,1,0:T(4,128)(2,1)S(1)} %reshape.76) | data formatting | bytes 2097152 | tf_op jit(solution)/shard_map/reshape | solution.py:112
  13.4 4.7 %all-to-all-start = ((bf16[2,64,4,1024]{3,1,0,2:T(8,128)(2,1)}), bf16[2,64,4,1024]{3,1,0,2:T(8,128)(2,1)S(1)}, u32[]{:S(2)}, u32[]{:S(2)}) async-start(bf16[2,64,4,1024]{3,1,0,2:T(8,128)(2,1)} %copy.15), calls=%async_computation | async-start | bytes 2097152 | tf_op jit(solution)/shard_map/all_to_all | solution.py:113
  18.8 25.5 %all-to-all-done = bf16[2,64,4,1024]{3,1,0,2:T(8,128)(2,1)S(1)} async-done(((bf16[2,64,4,1024]{3,1,0,2:T(8,128)(2,1)}), bf16[2,64,4,1024]{3,1,0,2:T(8,128)(2,1)S(1)}, u32[]{:S(2)}, u32[]{:S(2)}) %all-to-all-start) | async-done | bytes 1048608 | tf_op jit(solution)/shard_map/all_to_all | solution.py:113
  44.4 1.1 %copy.17 = bf16[2,256,1024]{1,0,2:T(2,128)(2,1)S(1)} copy(bf16[2,256,1024]{2,1,0:T(8,128)(2,1)S(1)} %bitcast.176) | data formatting | bytes 2097152 | tf_op jit(solution)/shard_map/squeeze | solution.py:114
  45.5 0.7 gather_fusion
  46.9 0.8 select_reduce_fusion
  48.7 0.9 add_reduce_fusion
  50.3 0.4 fusion.25
  51.0 0.4 multiply_reduce_fusion.1
  51.5 0.4 convolution_add_fusion.12
  51.8 0.4 fusion.79
  52.6 0.4 fusion.80
  55.4 0.4 fusion.78
  55.8 0.4 fusion.77
  56.2 0.4 fusion.11
  57.0 0.4 fusion.10
  58.5 0.4 fusion.75
  59.0 0.4 fusion.76
  59.4 0.4 fusion.8
  60.2 0.4 fusion.9
  61.7 0.6 fusion.74
  62.3 0.4 fusion.73
  62.8 0.4 fusion.7
  63.5 0.4 fusion.6
  65.1 0.4 fusion.71
  65.5 0.4 fusion.72
  65.9 0.4 fusion.4
  66.3 0.4 fusion.5
  68.2 0.4 fusion.27
  68.6 0.4 fusion.28
  69.0 0.4 fusion.18
  69.4 0.4 fusion.17
  72.1 3.1 %collective-permute-start.4 = (bf16[2,256,2,128]{3,2,1,0:T(2,128)(2,1)S(1)}, bf16[2,256,2,128]{3,2,1,0:T(2,128)(2,1)S(1)}, u32[]{:S(2)}, u32[]{:S(2)}) collective-permute-start(bf16[2,256,2,128]{3,2,1,0:T(2,128)(2,1)S(1)} %get-tuple-element.6), channel_id=1, source_target_pairs={{8,0},{16,8},{24,16},{0,24},{9,1},{17,9},{25,17},{1,25},{10,2},{18... | collective-permute-start | bytes 786440 | tf_op jit(solution)/shard_map/ppermute | solution.py:20
  75.2 5.9 %collective-permute-done.2 = bf16[2,256,2,128]{3,2,1,0:T(2,128)(2,1)S(1)} collective-permute-done((bf16[2,256,2,128]{3,2,1,0:T(2,128)(2,1)S(1)}, bf16[2,256,2,128]{3,2,1,0:T(2,128)(2,1)S(1)}, u32[]{:S(2)}, u32[]{:S(2)}) %collective-permute-start.2) | collective-permute-done | bytes 262176 | tf_op jit(solution)/shard_map/ppermute | solution.py:17
  81.1 4.5 %collective-permute-start.3 = (bf16[2,256,2,128]{3,2,1,0:T(2,128)(2,1)S(1)}, bf16[2,256,2,128]{3,2,1,0:T(2,128)(2,1)S(1)}, u32[]{:S(2)}, u32[]{:S(2)}) collective-permute-start(bf16[2,256,2,128]{3,2,1,0:T(2,128)(2,1)S(1)} %collective-permute-done.2), channel_id=1, source_target_pairs={{0,1},{1,2},{2,3},{3,4},{4,5},{5,6},{6,7},{8,9},{9,10},{10,11},{11... | collective-permute-start | bytes 786440 | tf_op jit(solution)/shard_map/ppermute | solution.py:28
  85.7 2.7 %collective-permute-start.5 = (bf16[2,256,2,128]{3,2,1,0:T(2,128)(2,1)S(1)}, bf16[2,256,2,128]{3,2,1,0:T(2,128)(2,1)S(1)}, u32[]{:S(2)}, u32[]{:S(2)}) collective-permute-start(bf16[2,256,2,128]{3,2,1,0:T(2,128)(2,1)S(1)} %collective-permute-done.4), channel_id=1, source_target_pairs={{1,0},{2,1},{3,2},{4,3},{5,4},{6,5},{7,6},{9,8},{10,9},{11,10},{12... | collective-permute-start | bytes 786440 | tf_op jit(solution)/shard_map/ppermute | solution.py:28
  88.4 0.5 collective-permute-done.3
  88.9 5.3 %collective-permute-done.5 = bf16[2,256,2,128]{3,2,1,0:T(2,128)(2,1)S(1)} collective-permute-done((bf16[2,256,2,128]{3,2,1,0:T(2,128)(2,1)S(1)}, bf16[2,256,2,128]{3,2,1,0:T(2,128)(2,1)S(1)}, u32[]{:S(2)}, u32[]{:S(2)}) %collective-permute-start.5) | collective-permute-done | bytes 262176 | tf_op jit(solution)/shard_map/ppermute | solution.py:28
  94.3 2.6 %add_convert_fusion = bf16[2,256,8,128]{3,2,1,0:T(8,128)(2,1)S(1)} fusion(bf16[2,256,8,128]{3,2,1,0:T(8,128)(2,1)S(1)} %bitcast_dynamic-update-slice_fusion, bf16[2,256,2,128]{3,2,1,0:T(2,128)(2,1)S(1)} %bitcast.185, bf16[2,256,2,128]{3,2,1,0:T(2,128)(2,1)S(1)} %bitcast.184, f32[256]{0:T(256)S(1)} %bitcast.192, f32[256]{0:T(256)S(1)} %bitcast.193, ...), kind=kLoop, calls=%fused_computation.5 | loop fusion | flops 14155776 | bytes 2626560 | tf_op jit(solution)/shard_map/convert_element_type | solution.py:94
  96.9 0.5 reshape.77
  97.9 10.8 %all_to_all.30 = f32[32,2,1,1024]{3,1,2,0:T(2,128)S(1)} all-to-all(f32[32,2,1,1024]{3,1,2,0:T(2,128)S(1)} %copy.18), channel_id=1, replica_groups=mesh['date'=4,'az'=8] {'date'}, dimensions={0} | all-to-all | bytes 524288 | tf_op jit(solution)/shard_map/all_to_all | solution.py:135
  108.9 0.8 reshape.78
  (66 shorter events, 13.6 us)
Async XLA Ops:
  0.0 97.4 %copy-start = (bf16[32,256]{1,0:T(8,128)(2,1)S(1)}, bf16[32,256]{1,0:T(8,128)(2,1)}, u32[]{:S(2)}) copy-start(bf16[32,256]{1,0:T(8,128)(2,1)} %param.11) | copy-start | bytes 49156
  0.0 10.0 %copy-start.1 = (bf16[2,64,32,128]{3,2,1,0:T(8,128)(2,1)S(1)}, bf16[2,64,32,128]{3,2,1,0:T(8,128)(2,1)}, u32[]{:S(2)}) copy-start(bf16[2,64,32,128]{3,2,1,0:T(8,128)(2,1)} %param.6) | copy-start | bytes 3145732
  1.2 8.7 %collective-permute-start.1 = (bf16[2,64,2,128]{3,2,1,0:T(2,128)(2,1)S(1)}, bf16[2,64,2,128]{3,2,1,0:T(2,128)(2,1)S(1)}, u32[]{:S(2)}, u32[]{:S(2)}) collective-permute-start(bf16[2,64,2,128]{3,2,1,0:T(2,128)(2,1)S(1)} %get-tuple-element.11), channel_id=1, source_target_pairs={{1,0},{2,1},{3,2},{4,3},{5,4},{6,5},{7,6},{9,8},{10,9},{11,10},{12... | collective-permute-start | bytes 196616 | tf_op jit(solution)/shard_map/ppermute | solution.py:20
  3.8 6.2 %collective-permute-start = (bf16[2,64,2,128]{3,2,1,0:T(2,128)(2,1)S(1)}, bf16[2,64,2,128]{3,2,1,0:T(2,128)(2,1)S(1)}, u32[]{:S(2)}, u32[]{:S(2)}) collective-permute-start(bf16[2,64,2,128]{3,2,1,0:T(2,128)(2,1)S(1)} %get-tuple-element.12), channel_id=1, source_target_pairs={{0,1},{1,2},{2,3},{3,4},{4,5},{5,6},{6,7},{8,9},{9,10},{10,11},{11... | collective-permute-start | bytes 196616 | tf_op jit(solution)/shard_map/ppermute | solution.py:17
  13.4 5.4 %copy-start.3 = (s32[1,1,64]{2,1,0:T(1,128)S(1)}, s32[1,1,64]{2,1,0:T(1,128)}, u32[]{:S(2)}) copy-start(s32[1,1,64]{2,1,0:T(1,128)} %param.8) | copy-start | bytes 772
  13.4 30.9 %all-to-all-start = ((bf16[2,64,4,1024]{3,1,0,2:T(8,128)(2,1)}), bf16[2,64,4,1024]{3,1,0,2:T(8,128)(2,1)S(1)}, u32[]{:S(2)}, u32[]{:S(2)}) async-start(bf16[2,64,4,1024]{3,1,0,2:T(8,128)(2,1)} %copy.15), calls=%async_computation | async-start | bytes 2097152 | tf_op jit(solution)/shard_map/all_to_all | solution.py:113
  71.4 0.7 copy-start.2
  71.9 9.3 %collective-permute-start.2 = (bf16[2,256,2,128]{3,2,1,0:T(2,128)(2,1)S(1)}, bf16[2,256,2,128]{3,2,1,0:T(2,128)(2,1)S(1)}, u32[]{:S(2)}, u32[]{:S(2)}) collective-permute-start(bf16[2,256,2,128]{3,2,1,0:T(2,128)(2,1)S(1)} %get-tuple-element.5), channel_id=1, source_target_pairs={{0,8},{8,16},{16,24},{24,0},{1,9},{9,17},{17,25},{25,1},{2,10},{10... | collective-permute-start | bytes 786440 | tf_op jit(solution)/shard_map/ppermute | solution.py:17
  72.1 13.6 %collective-permute-start.4 = (bf16[2,256,2,128]{3,2,1,0:T(2,128)(2,1)S(1)}, bf16[2,256,2,128]{3,2,1,0:T(2,128)(2,1)S(1)}, u32[]{:S(2)}, u32[]{:S(2)}) collective-permute-start(bf16[2,256,2,128]{3,2,1,0:T(2,128)(2,1)S(1)} %get-tuple-element.6), channel_id=1, source_target_pairs={{8,0},{16,8},{24,16},{0,24},{9,1},{17,9},{25,17},{1,25},{10,2},{18... | collective-permute-start | bytes 786440 | tf_op jit(solution)/shard_map/ppermute | solution.py:20
  81.1 7.8 %collective-permute-start.3 = (bf16[2,256,2,128]{3,2,1,0:T(2,128)(2,1)S(1)}, bf16[2,256,2,128]{3,2,1,0:T(2,128)(2,1)S(1)}, u32[]{:S(2)}, u32[]{:S(2)}) collective-permute-start(bf16[2,256,2,128]{3,2,1,0:T(2,128)(2,1)S(1)} %collective-permute-done.2), channel_id=1, source_target_pairs={{0,1},{1,2},{2,3},{3,4},{4,5},{5,6},{6,7},{8,9},{9,10},{10,11},{11... | collective-permute-start | bytes 786440 | tf_op jit(solution)/shard_map/ppermute | solution.py:28
  85.7 8.6 %collective-permute-start.5 = (bf16[2,256,2,128]{3,2,1,0:T(2,128)(2,1)S(1)}, bf16[2,256,2,128]{3,2,1,0:T(2,128)(2,1)S(1)}, u32[]{:S(2)}, u32[]{:S(2)}) collective-permute-start(bf16[2,256,2,128]{3,2,1,0:T(2,128)(2,1)S(1)} %collective-permute-done.4), channel_id=1, source_target_pairs={{1,0},{2,1},{3,2},{4,3},{5,4},{6,5},{7,6},{9,8},{10,9},{11,10},{12... | collective-permute-start | bytes 786440 | tf_op jit(solution)/shard_map/ppermute | solution.py:28
where the time goes:
time: 110 us
  waiting for transfers between devices  37.3 us (34%)
  matrix products  23.1 us (21%)
  starting transfers between devices  21.5 us (20%)
  blocking collectives  10.8 us (10%)
  local copies, waits for them, and re-layouts  9.66 us (9%)
  other arithmetic  4.7 us (4%)
  between operations  2.7 us (2%)
    all_to_all x1, waiting for transfers between devices, on_device(): lax.all_to_all(grouped, 'date', split_axis=2, concat_axis=1, tiled=True)  25.5 us
    all_to_all x1, blocking collectives, on_device(): lax.all_to_all(whole[:, :, None, :], 'date', split_axis=0, concat_axis=2,...  10.8 us
    ppermute x2, starting transfers between devices, shifted(): return lax.ppermute(shard, axis, pairs)  7.14 us
    ppermute x2, waiting for transfers between devices, padded_2(): lax.ppermute(lax.slice_in_dim(block, block.shape[dim] - width, None, axis...  5.93 us
    ppermute x2, waiting for transfers between devices, shifted(): return lax.ppermute(shard, axis, pairs)  5.86 us
    ppermute x2, starting transfers between devices, padded_2(): lax.ppermute(lax.slice_in_dim(block, 0, width, axis=dim), axis, backward)  5.66 us
    dot_general x13, matrix products, complex_product(): jnp.dot(left_re, right_re, precision=highest)  5.31 us
    dot_general x13, matrix products, complex_product(): jnp.dot(left_re, right_im, precision=highest)  5.05 us
  transfers between devices with their start and end apart: 7, of which 4 were waited for; matrix products, arithmetic and copies ran while one was open for 2% of the time, Pallas kernels for 0%

commit v1 on v0

v1 whole, which is shorter than its diff:
```python
import functools

import jax
import jax.numpy as jnp
import numpy as np
from jax import lax
from jax.experimental import pallas as pl
from jax.experimental.pallas import tpu as pltpu
from jax.sharding import PartitionSpec as P

NS_ITERS = 6
SMOOTH_REACH = 2
MESH = pl.DeviceIdType.MESH
HIGHEST = lax.Precision.HIGHEST
F32 = jnp.float32
BF16 = jnp.bfloat16


def exact_dot(left, right):
    return jnp.dot(left, right, precision=HIGHEST, preferred_element_type=F32)


def project_gain(what, weight, masked, scales, looks):
    dates2, width = what.shape
    dates = dates2 // 2
    gram = lax.dot_general(what, what, (((0,), (0,)), ((), ())), preferred_element_type=F32)
    line = lax.broadcasted_iota(jnp.int32, (width, width), 0)
    column = lax.broadcasted_iota(jnp.int32, (width, width), 1)
    eye = (line == column).astype(F32)

    def total(array):
        return jnp.sum(jnp.sum(array, axis=1, keepdims=True), axis=0, keepdims=True)

    trace = total(gram * eye) * 0.5
    mu = trace / (looks * dates) + 1e-06
    alpha = (1.0 - weight) / looks
    c = (1.0 + weight) * mu
    core = alpha * gram
    square = total(core * core) * 0.5 + 2.0 * c * alpha * trace + c * c * dates
    scale = 1.0 / jnp.sqrt(square)
    rho = 1.0 - scale * c
    r = rho * eye - scale * core
    first = r
    dr = -scale * (rho * eye + first)
    df = -scale * eye
    f0 = 1.0 + rho
    r = exact_dot(first, first)
    rho = rho * rho
    for step in range(1, NS_ITERS):
        if step == NS_ITERS - 1:
            df = f0 * dr + df + exact_dot(df, r)
            f0 = f0 * (1.0 + rho)
        elif step == 1:
            out = exact_dot(jnp.concatenate([dr, r], axis=0), r)
            df = f0 * dr + df - scale * r
            f0 = f0 * (1.0 + rho)
            dr = rho * dr + out[:width]
            r = out[width:]
            rho = rho * rho
        else:
            out = exact_dot(jnp.concatenate([df, dr, r], axis=0), r)
            df = f0 * dr + df + out[:width]
            f0 = f0 * (1.0 + rho)
            dr = rho * dr + out[width : 2 * width]
            r = out[2 * width :]
            rho = rho * rho
    inner = scale * (f0 * eye + weight * mu * df + exact_dot(core, df))
    base = weight * mu * scale * f0
    seen = lax.dot_general(what[:dates], masked, (((0,), (1,)), ((), ())), preferred_element_type=F32)
    small = exact_dot(inner, alpha * seen)
    both = exact_dot(what.astype(F32), small)
    real = (both[:dates] + base * jnp.transpose(masked.astype(F32))) * scales
    imag = both[dates:] * scales
    return real.astype(BF16), imag.astype(BF16)


def kernel(
    groups, slabs, looks, taps_count, unit,
    x_ref, taps_ref, idx_ref, weight_ref, masked_ref, scales_ref, order_ref, out_ref,
    halo, idx_all, z, wsend, what, vsend, vrecv, u, psend, precv, esend, erecv,
    s_halo, r_halo, s_idx, r_idx, s_w, r_w, s_v, r_v, s_p, r_p, s_e, r_e,
):
    me = lax.axis_index("date")
    az = lax.axis_index("az")
    rows, dates2, cols = x_ref.shape
    dates = dates2 // 2
    block_rows = rows // groups
    reach = taps_count // 2
    classes = SMOOTH_REACH + 1
    has_low = az > 0
    has_high = az < slabs - 1

    barrier = pltpu.get_barrier_semaphore()
    peers = [lax.rem(me + o, groups) for o in range(groups)]

    def greet(d, a):
        pl.semaphore_signal(barrier, inc=1, device_id={"date": d, "az": a}, device_id_type=MESH)

    for o in range(1, groups):
        greet(peers[o], az)

    @pl.when(has_low)
    def _():
        for o in range(groups):
            greet(peers[o], az - 1)

    @pl.when(has_high)
    def _():
        for o in range(groups):
            greet(peers[o], az + 1)

    pl.semaphore_wait(
        barrier,
        groups - 1 + groups * (has_low.astype(jnp.int32) + has_high.astype(jnp.int32)),
    )

    def remote(src, dst, send, recv, d, a):
        return pltpu.make_async_remote_copy(
            src_ref=src, dst_ref=dst, send_sem=send, recv_sem=recv,
            device_id={"date": d, "az": a}, device_id_type=MESH,
        )

    def halo_down():
        return remote(x_ref.at[pl.ds(0, reach)], halo.at[1], s_halo.at[0], r_halo.at[1], me, az - 1)

    def halo_up():
        return remote(
            x_ref.at[pl.ds(rows - reach, reach)], halo.at[0], s_halo.at[1], r_halo.at[0], me, az + 1
        )

    def idx_copy(o, src):
        return remote(idx_ref, idx_all.at[src], s_idx.at[o], r_idx.at[src], peers[o], az)

    pl.when(has_low)(lambda: halo_down().start())
    pl.when(has_high)(lambda: halo_up().start())
    for o in range(1, groups):
        idx_copy(o, me).start()
    idx_all[me] = idx_ref[...]

    def fir(b, i, row_of):
        total = None
        for j in range(taps_count):
            term = taps_ref[:, j : j + 1] * row_of(i + j - reach).astype(F32)
            total = term if total is None else total + term
        z[b, :, i * cols : (i + 1) * cols] = total.astype(BF16)

    @pl.loop(0, groups)
    def _(b):
        for i in range(block_rows):
            if reach <= i < block_rows - reach:
                fir(b, i, lambda q: x_ref[b * block_rows + q])

    @pl.loop(0, groups - 1)
    def _(b):
        for i in range(block_rows - reach, block_rows):
            fir(b, i, lambda q: x_ref[b * block_rows + q])
        for i in range(reach):
            fir(b + 1, i, lambda q: x_ref[(b + 1) * block_rows + q])

    @pl.when(has_low)
    def _():
        halo_up().wait_recv()

    @pl.when(jnp.logical_not(has_low))
    def _():
        halo[0] = jnp.zeros(halo.shape[1:], BF16)

    @pl.when(has_high)
    def _():
        halo_down().wait_recv()

    @pl.when(jnp.logical_not(has_high))
    def _():
        halo[1] = jnp.zeros(halo.shape[1:], BF16)

    for i in range(reach):
        fir(0, i, lambda q: x_ref[q] if q >= 0 else halo[0, reach + q])
    last = (groups - 1) * block_rows
    for i in range(block_rows - reach, block_rows):
        fir(
            groups - 1, i,
            lambda q: x_ref[last + q] if q < block_rows else halo[1, q - block_rows],
        )

    def w_copy(o, src):
        return remote(
            wsend.at[peers[o]],
            what.at[:, pl.ds(pl.multiple_of(src * dates, dates), dates), :],
            s_w.at[o], r_w.at[src], peers[o], az,
        )

    for o in list(range(1, groups)) + [0]:
        b = peers[o]
        if o:
            idx_copy(o, b).wait_recv()
        chosen = idx_all[b][0:1, :]
        pixel = lax.broadcasted_iota(jnp.int32, (block_rows * cols, 2 * looks), 0)
        pick = (pixel == chosen).astype(F32).astype(BF16)
        sample = jnp.dot(z[b], pick, preferred_element_type=F32)
        left = lax.broadcasted_iota(jnp.int32, (dates, 2 * looks), 1) < looks
        real, imag = sample[:dates], sample[dates:]
        top = jnp.where(left, real, -imag).astype(BF16)
        bottom = jnp.where(left, imag, real).astype(BF16)
        if o:
            wsend[b, 0] = top
            wsend[b, 1] = bottom
            w_copy(o, me).start()
        else:
            own = pl.ds(pl.multiple_of(me * dates, dates), dates)
            what[0, own, :] = top
            what[1, own, :] = bottom
    for o in range(1, groups):
        w_copy(o, peers[o]).wait_recv()

    whole = what[...].reshape(2 * groups * dates, 2 * looks)
    real, imag = project_gain(whole, weight_ref[0:1, 0:1], masked_ref[...], scales_ref[0:1, :], looks)
    vsend[0] = real
    vsend[1] = imag

    def v_copy(o, src):
        return remote(
            vsend.at[:, pl.ds(pl.multiple_of(peers[o] * dates, dates), dates), :],
            vrecv.at[src], s_v.at[o], r_v.at[src], peers[o], az,
        )

    for o in range(1, groups):
        v_copy(o, me).start()
    vrecv[me] = vsend[:, pl.ds(pl.multiple_of(me * dates, dates), dates), :]

    zeros = jnp.zeros((SMOOTH_REACH,) + u.shape[1:], F32)
    u[0:SMOOTH_REACH] = zeros
    u[rows + SMOOTH_REACH : rows + 2 * SMOOTH_REACH] = zeros
    for o in range(groups):
        b = peers[o]
        if o:
            v_copy(o, b).wait_recv()
        v_re = vrecv[b, 0]
        v_im = vrecv[b, 1]
        upper = jnp.concatenate([v_re, v_im], axis=0)
        lower = jnp.concatenate([-v_im, v_re], axis=0)
        mix = lax.dot_general(
            order_ref[...], jnp.concatenate([upper, lower], axis=1),
            (((1,), (1,)), ((), ())), preferred_element_type=F32,
        ).astype(BF16)
        found = jnp.dot(mix, z[b], preferred_element_type=F32)
        for i in range(block_rows):
            u[SMOOTH_REACH + b * block_rows + i] = found[:, i * cols : (i + 1) * cols]

    def smooth(r, d, place):
        total = None
        for h in range(classes):
            at = pl.ds(pl.multiple_of((h * groups + d) * unit, 8), unit)
            for j in range(-h, h + 1):
                if place is None or 0 <= place + j < rows:
                    term = u[r + j + SMOOTH_REACH, at, :]
                    total = term if total is None else total + term
        return total

    def e_copy(side, o, src, target):
        return remote(
            esend.at[side, peers[o]], erecv.at[1 - side, src],
            s_e.at[side, o], r_e.at[1 - side, src], peers[o], target,
        )

    for o in range(groups):
        d = peers[o]
        for i in range(SMOOTH_REACH):
            esend[0, d, i] = smooth(i - SMOOTH_REACH, d, i - SMOOTH_REACH).astype(BF16)
            esend[1, d, i] = smooth(rows + i, d, rows + i).astype(BF16)
        pl.when(has_low)(lambda o=o: e_copy(0, o, me, az - 1).start())
        pl.when(has_high)(lambda o=o: e_copy(1, o, me, az + 1).start())

    def p_copy(o, src):
        return remote(psend.at[peers[o]], precv.at[src], s_p.at[o], r_p.at[src], peers[o], az)

    for o in range(1, groups):
        d = peers[o]

        @pl.loop(0, rows)
        def _(r):
            psend[d, r] = smooth(r, d, None).astype(BF16)

        p_copy(o, me).start()

    @pl.loop(0, rows)
    def _(r):
        out_ref[r] = smooth(r, me, None)

    @pl.when(has_low)
    def _():
        for o in range(groups):
            e_copy(1, o, peers[o], az - 1).wait_recv()
        for i in range(SMOOTH_REACH):
            for o in range(groups):
                out_ref[i] += erecv[0, peers[o], i].astype(F32)

    @pl.when(has_high)
    def _():
        for o in range(groups):
            e_copy(0, o, peers[o], az + 1).wait_recv()
        for i in range(SMOOTH_REACH):
            for o in range(groups):
                out_ref[rows - SMOOTH_REACH + i] += erecv[1, peers[o], i].astype(F32)

    for o in range(1, groups):
        p_copy(o, peers[o]).wait_recv()
        out_ref[...] += precv[peers[o]].astype(F32)

    pl.when(has_low)(lambda: halo_down().wait_send())
    pl.when(has_high)(lambda: halo_up().wait_send())
    for o in range(groups):
        if o:
            idx_copy(o, me).wait_send()
            w_copy(o, me).wait_send()
            v_copy(o, me).wait_send()
            p_copy(o, me).wait_send()
        pl.when(has_low)(lambda o=o: e_copy(0, o, me, az - 1).wait_send())
        pl.when(has_high)(lambda o=o: e_copy(1, o, me, az + 1).wait_send())


def on_device(slc_stack, fir_taps, look_index, shrink_level, window_half, basis):
    parts, dates, rows, cols = slc_stack.shape
    groups = lax.axis_size("date")
    slabs = lax.axis_size("az")
    taps_count = fir_taps.shape[1]
    looks = look_index.shape[2]
    bases, all_dates = basis.shape
    own = bases // groups
    unit = -(-2 * own // 8) * 8
    classes = SMOOTH_REACH + 1

    x = slc_stack.transpose(2, 0, 1, 3).reshape(rows, parts * dates, cols)
    taps = jnp.concatenate([fir_taps, fir_taps], axis=0)
    chosen = look_index.reshape(1, looks)
    chosen = jnp.broadcast_to(jnp.concatenate([chosen, chosen], axis=1), (8, 2 * looks))
    weight = jnp.broadcast_to(shrink_level.astype(F32) / 16.0, (8, 128))
    inside = window_half[None, :] == jnp.arange(classes)[:, None]
    masked = jnp.where(inside[:, None, :], basis[None], jnp.zeros_like(basis)[None])
    masked = masked.reshape(classes * bases, all_dates)
    filled = -(-masked.shape[0] // 128) * 128
    masked = jnp.pad(masked, ((0, filled - masked.shape[0]), (0, 0)))
    scales = jnp.repeat(1.0 / (2.0 * jnp.arange(classes, dtype=F32) + 1.0), bases)
    scales = jnp.broadcast_to(jnp.pad(scales, (0, filled - scales.shape[0])), (8, filled))
    order_rows = np.zeros((classes, groups, unit, 2, filled), np.float32)
    for h in range(classes):
        for d in range(groups):
            for part in range(2):
                for k in range(own):
                    order_rows[h, d, part * own + k, part, h * bases + d * own + k] = 1.0
    order_rows = jnp.asarray(order_rows.reshape(classes * groups * unit, 2 * filled), BF16)

    block_rows = rows // groups
    dma = pltpu.SemaphoreType.DMA
    vmem = pl.BlockSpec(memory_space=pltpu.VMEM)
    scratch = [
        pltpu.VMEM((2, taps_count // 2, 2 * dates, cols), BF16),
        pltpu.VMEM((groups, 8, 2 * looks), jnp.int32),
        pltpu.VMEM((groups, 2 * dates, block_rows * cols), BF16),
        pltpu.VMEM((groups, 2, dates, 2 * looks), BF16),
        pltpu.VMEM((2, all_dates, 2 * looks), BF16),
        pltpu.VMEM((2, all_dates, filled), BF16),
        pltpu.VMEM((groups, 2, dates, filled), BF16),
        pltpu.VMEM((rows + 2 * SMOOTH_REACH, classes * groups * unit, cols), F32),
        pltpu.VMEM((groups, rows, unit, cols), BF16),
        pltpu.VMEM((groups, rows, unit, cols), BF16),
        pltpu.VMEM((2, groups, SMOOTH_REACH, unit, cols), BF16),
        pltpu.VMEM((2, groups, SMOOTH_REACH, unit, cols), BF16),
        dma((2,)), dma((2,)),
        dma((groups,)), dma((groups,)),
        dma((groups,)), dma((groups,)),
        dma((groups,)), dma((groups,)),
        dma((groups,)), dma((groups,)),
        dma((2, groups)), dma((2, groups)),
    ]
    out = pl.pallas_call(
        functools.partial(kernel, groups, slabs, looks, taps_count, unit),
        out_shape=jax.ShapeDtypeStruct((rows, unit, cols), F32),
        in_specs=[vmem] * 7,
        out_specs=vmem,
        scratch_shapes=scratch,
        compiler_params=pltpu.CompilerParams(
            collective_id=0, has_side_effects=True, vmem_limit_bytes=60 * 2**20
        ),
    )(x, taps, chosen, weight, masked, scales, order_rows)
    out = out[:, : 2 * own].reshape(rows, 2, own, cols)
    return out.transpose(2, 1, 0, 3)


def solution(mesh):
    in_specs = (
        P(None, "date", "az", None),
        P("date", None),
        P("az", "date", None),
        P("az", "date"),
        P(),
        P(),
    )
    out_specs = P("date", None, "az", None)
    return jax.shard_map(
        on_device, mesh=mesh, in_specs=in_specs, out_specs=out_specs, check_vma=False
    )
```

time: 110 us -> 48.2 us (0.44)
  the two profiles are of different devices: /device:TPU:3 before, /device:TPU:10 now
where the time goes in v1:
time: 48.2 us; the launch traced here: 47.9 us
  Pallas kernels  38.2 us (79%)
  local copies, waits for them, and re-layouts  8.89 us (18%)
  between operations  0.69 us (1%)
    pallas_call x1, Pallas kernels, on_device(): pl.pallas_call(functools.partial(kernel, groups, slabs, looks, taps_count...  38.2 us
    transpose x1, local copies, waits for them, and re-layouts, on_device(): x = slc_stack.transpose(2, 0, 1, 3).reshape(rows, parts * dates, cols)  2.6 us
    reshape x1, local copies, waits for them, and re-layouts, on_device(): out = out[:, :2 * own].reshape(rows, 2, own, cols)  1.74 us
    unnamed x8, local copies, waits for them, and re-layouts  1.25 us

profile of v1, /device:TPU:10, one launch (start us, length us, event | category | flops | bytes accessed | tf_op | source)
XLA Modules:
  0.0 47.9 jit_solution(6920745460652248766)
XLA Ops:
  0.7 0.0 copy-start.3
  0.7 0.6 %copy-done.3 = s32[1,1,64]{2,1,0:T(1,128)S(1)} copy-done((s32[1,1,64]{2,1,0:T(1,128)S(1)}, s32[1,1,64]{2,1,0:T(1,128)}, u32[]{:S(2)}) %copy-start.3) | copy-done | bytes 280
  1.3 0.0 copy-start.2
  1.3 0.1 add_bitcast_fusion
  1.4 0.0 copy-start
  1.4 0.6 %copy-done.2 = s32[256]{0:T(256)S(1)} copy-done((s32[256]{0:T(256)S(1)}, s32[256]{0:T(256)}, u32[]{:S(2)}) %copy-start.2) | copy-done | bytes 1048
  2.0 0.1 broadcast_in_dim.55
  2.1 0.1 reshape.38
  2.2 0.6 %broadcast_in_dim.56.scales_ref = f32[8,128]{1,0:T(8,128)} broadcast(f32[128]{0:T(128)S(1)} %pad.9), dimensions={1} | broadcast | bytes 4608 | tf_op jit(solution)/shard_map/broadcast_in_dim | solution.py:343
  2.8 0.0 copy-start.1
  2.8 0.6 %broadcast_in_dim.49.idx_ref = s32[8,128]{1,0:T(8,128)} broadcast(s32[128]{0:T(128)S(1)} %add_bitcast_fusion), dimensions={1} | broadcast | bytes 4608 | tf_op jit(solution)/shard_map/broadcast_in_dim | solution.py:335
  3.4 0.6 %broadcast_in_dim.51.weight_ref = f32[8,128]{1,0:T(8,128)} broadcast(f32[]{:T(128)} %bitcast.4), dimensions={} | broadcast | bytes 4100 | tf_op jit(solution)/shard_map/broadcast_in_dim | solution.py:336
  3.9 0.0 copy-done.1
  3.9 0.1 pad_maximum_fusion
  4.0 0.0 copy-done
  4.0 0.6 %pad.8.masked_ref = bf16[128,256]{1,0:T(8,128)(2,1)} pad(bf16[96,256]{1,0:T(8,128)(2,1)S(1)} %bitcast.14, bf16[]{:T(256)} %constant.5.clone.1), padding=0_32x0_0 | pad | bytes 114690 | tf_op jit(solution)/shard_map/jit(_pad)/pad | solution.py:341
  4.7 0.7 %copy.13.taps_ref = f32[128,5]{1,0:T(8,128)} copy(f32[128,5]{0,1:T(8,128)S(1)} %pad_maximum_fusion) | data formatting | bytes 5120 | tf_op jit(solution)/shard_map/concatenate | solution.py:333
  5.4 2.6 %copy.12 = bf16[32,2,64,128]{3,2,1,0:T(8,128)(2,1)} copy(bf16[32,2,64,128]{3,0,2,1:T(8,128)(2,1)} %bitcast.12) | data formatting | bytes 2097152 | tf_op jit(solution)/shard_map/transpose | solution.py:332
  8.0 38.2 %shard_map.73 = f32[32,16,128]{2,1,0:T(8,128)} custom-call(bf16[32,128,128]{2,1,0:T(8,128)(2,1)} %bitcast.11, f32[128,5]{1,0:T(8,128)} %copy.13.taps_ref, s32[8,128]{1,0:T(8,128)} %broadcast_in_dim.49.idx_ref, f32[8,128]{1,0:T(8,128)} %broadcast_in_dim.51.weight_ref, bf16[128,256]{1,0:T(8,128)(2,1)} %pad.8.masked_ref, f32[8,128]{1,0:T(8,128)} %broadcast_in_dim.56.scales_ref, ...), custom_call_target="tpu_custom_call" | custom-call | tf_op jit(solution)/shard_map/pallas_call | solution.py:375
  46.2 1.7 %copy.16 = f32[32,2,8,128]{3,0,1,2:T(8,128)} copy(f32[32,2,8,128]{3,2,1,0:T(8,128)} %bitcast.13) | data formatting | bytes 524288 | tf_op jit(solution)/shard_map/reshape | solution.py:385
  (4 shorter events, 0.0 us)
Async XLA Ops:
  0.7 0.7 %copy-start.3 = (s32[1,1,64]{2,1,0:T(1,128)S(1)}, s32[1,1,64]{2,1,0:T(1,128)}, u32[]{:S(2)}) copy-start(s32[1,1,64]{2,1,0:T(1,128)} %param.9) | copy-start | bytes 772
  1.3 0.7 %copy-start.2 = (s32[256]{0:T(256)S(1)}, s32[256]{0:T(256)}, u32[]{:S(2)}) copy-start(s32[256]{0:T(256)} %param.11) | copy-start | bytes 3076
  1.4 2.6 %copy-start = (bf16[32,256]{1,0:T(8,128)(2,1)S(1)}, bf16[32,256]{1,0:T(8,128)(2,1)}, u32[]{:S(2)}) copy-start(bf16[32,256]{1,0:T(8,128)(2,1)} %param.12) | copy-start | bytes 49156
  2.8 1.2 %copy-start.1 = (f32[64,5]{0,1:T(8,128)S(1)}, f32[64,5]{0,1:T(8,128)}, u32[]{:S(2)}) copy-start(f32[64,5]{0,1:T(8,128)} %param.8) | copy-start | bytes 3844

commit v2 on v1

--- a/solution.py
+++ b/solution.py
@@ -2,7 +2,6 @@
 
 import jax
 import jax.numpy as jnp
-import numpy as np
 from jax import lax
 from jax.experimental import pallas as pl
 from jax.experimental.pallas import tpu as pltpu
@@ -20,70 +19,91 @@
     return jnp.dot(left, right, precision=HIGHEST, preferred_element_type=F32)
 
 
-def project_gain(what, weight, masked, scales, looks):
+def split_dot(left, right):
+    high = right.astype(BF16)
+    low = (right - high.astype(F32)).astype(BF16)
+    both = lax.dot_general(
+        left, jnp.concatenate([high, low], axis=0), (((1,), (1,)), ((), ())),
+        preferred_element_type=F32,
+    )
+    return both[:, : right.shape[0]] + both[:, right.shape[0] :]
+
+
+def project_gain(what, weight, masked, turned, scales, looks):
     dates2, width = what.shape
     dates = dates2 // 2
     gram = lax.dot_general(what, what, (((0,), (0,)), ((), ())), preferred_element_type=F32)
     line = lax.broadcasted_iota(jnp.int32, (width, width), 0)
     column = lax.broadcasted_iota(jnp.int32, (width, width), 1)
     eye = (line == column).astype(F32)
+    left = lax.broadcasted_iota(jnp.int32, (looks, width), 1) < looks
 
     def total(array):
         return jnp.sum(jnp.sum(array, axis=1, keepdims=True), axis=0, keepdims=True)
 
+    def full(top):
+        turn = pltpu.roll(top, looks, 1)
+        return jnp.concatenate([top, jnp.where(left, -turn, turn)], axis=0)
+
     trace = total(gram * eye) * 0.5
+    norm = total(gram * gram) * 0.5
     mu = trace / (looks * dates) + 1e-06
     alpha = (1.0 - weight) / looks
     c = (1.0 + weight) * mu
     core = alpha * gram
-    square = total(core * core) * 0.5 + 2.0 * c * alpha * trace + c * c * dates
+    square = alpha * alpha * norm + 2.0 * c * alpha * trace + c * c * dates
     scale = 1.0 / jnp.sqrt(square)
     rho = 1.0 - scale * c
-    r = rho * eye - scale * core
-    first = r
-    dr = -scale * (rho * eye + first)
+    whole = rho * eye - scale * core
+    eye = eye[:looks]
+    r = whole[:looks]
+    dr = -scale * (rho * eye + r)
     df = -scale * eye
     f0 = 1.0 + rho
-    r = exact_dot(first, first)
+    r = exact_dot(r, whole)
     rho = rho * rho
     for step in range(1, NS_ITERS):
+        whole = full(r)
         if step == NS_ITERS - 1:
-            df = f0 * dr + df + exact_dot(df, r)
+            df = f0 * dr + df + exact_dot(df, whole)
             f0 = f0 * (1.0 + rho)
         elif step == 1:
-            out = exact_dot(jnp.concatenate([dr, r], axis=0), r)
+            out = exact_dot(jnp.concatenate([dr, r], axis=0), whole)
             df = f0 * dr + df - scale * r
             f0 = f0 * (1.0 + rho)
-            dr = rho * dr + out[:width]
-            r = out[width:]
+            dr = rho * dr + out[:looks]
+            r = out[looks:]
             rho = rho * rho
         else:
-            out = exact_dot(jnp.concatenate([df, dr, r], axis=0), r)
-            df = f0 * dr + df + out[:width]
+            out = exact_dot(jnp.concatenate([df, dr, r], axis=0), whole)
+            df = f0 * dr + df + out[:looks]
             f0 = f0 * (1.0 + rho)
-            dr = rho * dr + out[width : 2 * width]
-            r = out[2 * width :]
+            dr = rho * dr + out[looks : 2 * looks]
+            r = out[2 * looks :]
             rho = rho * rho
-    inner = scale * (f0 * eye + weight * mu * df + exact_dot(core, df))
+    inner = full(scale * (f0 * eye + weight * mu * df + exact_dot(df, core)))
     base = weight * mu * scale * f0
-    seen = lax.dot_general(what[:dates], masked, (((0,), (1,)), ((), ())), preferred_element_type=F32)
-    small = exact_dot(inner, alpha * seen)
-    both = exact_dot(what.astype(F32), small)
-    real = (both[:dates] + base * jnp.transpose(masked.astype(F32))) * scales
+    seen = jnp.dot(masked, what[:dates], preferred_element_type=F32)
+    small = exact_dot(alpha * seen, inner)
+    both = split_dot(what, small)
+    real = (both[:dates] + base * turned) * scales
     imag = both[dates:] * scales
     return real.astype(BF16), imag.astype(BF16)
 
 
 def kernel(
-    groups, slabs, looks, taps_count, unit,
-    x_ref, taps_ref, idx_ref, weight_ref, masked_ref, scales_ref, order_ref, out_ref,
-    halo, idx_all, z, wsend, what, vsend, vrecv, u, psend, precv, esend, erecv,
+    groups, slabs, unit, own, pitch, filled,
+    x_ref, taps_ref, look_ref, level_ref, window_ref, basis_ref, out_ref,
+    xf, halo_send, halo, idx_send, idx_all, masked_ref, turned_ref, order_ref,
+    z, wsend, what, vsend, vrecv, u, psend, precv, esend, erecv,
     s_halo, r_halo, s_idx, r_idx, s_w, r_w, s_v, r_v, s_p, r_p, s_e, r_e,
 ):
     me = lax.axis_index("date")
     az = lax.axis_index("az")
-    rows, dates2, cols = x_ref.shape
-    dates = dates2 // 2
+    _, dates, rows, cols = x_ref.shape
+    taps_count = taps_ref.shape[1]
+    looks = look_ref.shape[1]
+    bases = basis_ref.shape[0]
     block_rows = rows // groups
     reach = taps_count // 2
     classes = SMOOTH_REACH + 1
@@ -109,6 +129,34 @@
         for o in range(groups):
             greet(peers[o], az + 1)
 
+    chosen = jnp.broadcast_to(look_ref[...], (8, looks))
+    idx_send[...] = jnp.concatenate([chosen, chosen], axis=1)
+
+    def widen(t):
+        for part in range(2):
+            at = pl.ds(pl.multiple_of((part * dates + t) * pitch, 8), rows)
+            xf[at, :] = x_ref[part, t].astype(F32)
+
+    @pl.loop(0, dates // 8)
+    def _(g):
+        for t in range(8):
+            widen(g * 8 + t)
+
+    def fir_rows(part, g):
+        first = part * dates + g * 16
+        return (
+            pl.ds(pl.multiple_of(first, 16), 16),
+            lambda r: xf[pl.ds(first * pitch + r, 16, stride=pitch), :],
+        )
+
+    @pl.loop(0, dates // 16)
+    def _(g):
+        for part in range(2):
+            at, row = fir_rows(part, g)
+            for q in range(reach):
+                halo_send[0, q, at, :] = row(q).astype(BF16)
+                halo_send[1, q, at, :] = row(rows - reach + q).astype(BF16)
+
     pl.semaphore_wait(
         barrier,
         groups - 1 + groups * (has_low.astype(jnp.int32) + has_high.astype(jnp.int32)),
@@ -121,41 +169,63 @@
         )
 
     def halo_down():
-        return remote(x_ref.at[pl.ds(0, reach)], halo.at[1], s_halo.at[0], r_halo.at[1], me, az - 1)
+        return remote(halo_send.at[0], halo.at[1], s_halo.at[0], r_halo.at[1], me, az - 1)
 
     def halo_up():
-        return remote(
-            x_ref.at[pl.ds(rows - reach, reach)], halo.at[0], s_halo.at[1], r_halo.at[0], me, az + 1
-        )
+        return remote(halo_send.at[1], halo.at[0], s_halo.at[1], r_halo.at[0], me, az + 1)
 
     def idx_copy(o, src):
-        return remote(idx_ref, idx_all.at[src], s_idx.at[o], r_idx.at[src], peers[o], az)
+        return remote(idx_send, idx_all.at[src], s_idx.at[o], r_idx.at[src], peers[o], az)
 
     pl.when(has_low)(lambda: halo_down().start())
     pl.when(has_high)(lambda: halo_up().start())
     for o in range(1, groups):
         idx_copy(o, me).start()
-    idx_all[me] = idx_ref[...]
-
-    def fir(b, i, row_of):
-        total = None
-        for j in range(taps_count):
-            term = taps_ref[:, j : j + 1] * row_of(i + j - reach).astype(F32)
-            total = term if total is None else total + term
-        z[b, :, i * cols : (i + 1) * cols] = total.astype(BF16)
-
-    @pl.loop(0, groups)
-    def _(b):
-        for i in range(block_rows):
-            if reach <= i < block_rows - reach:
-                fir(b, i, lambda q: x_ref[b * block_rows + q])
-
-    @pl.loop(0, groups - 1)
-    def _(b):
-        for i in range(block_rows - reach, block_rows):
-            fir(b, i, lambda q: x_ref[b * block_rows + q])
-        for i in range(reach):
-            fir(b + 1, i, lambda q: x_ref[(b + 1) * block_rows + q])
+    idx_all[me] = idx_send[...]
+
+    def taps_of(g):
+        taps = taps_ref[pl.ds(pl.multiple_of(g * 16, 16), 16), :]
+        return [jnp.broadcast_to(taps[:, j : j + 1], (16, cols)) for j in range(taps_count)]
+
+    def fir(r, at, taps, window):
+        total = taps[0] * window[0]
+        for j in range(1, taps_count):
+            total = total + taps[j] * window[j]
+        b, i = r // block_rows, r % block_rows
+        z[b, at, i * cols : (i + 1) * cols] = total.astype(BF16)
+
+    @pl.loop(0, dates // 16)
+    def _(g):
+        taps = taps_of(g)
+        for part in range(2):
+            at, row = fir_rows(part, g)
+            window = [row(r) for r in range(2 * reach)]
+            for r in range(reach, rows - reach):
+                window = window[-2 * reach :] + [row(r + reach)]
+                fir(r, at, taps, window)
+
+    zeros = jnp.zeros((SMOOTH_REACH,) + u.shape[1:], F32)
+    u[0:SMOOTH_REACH] = zeros
+    u[rows + SMOOTH_REACH : rows + 2 * SMOOTH_REACH] = zeros
+    basis = basis_ref[...].astype(F32)
+    masked = [jnp.where(window_ref[...] == h, basis, 0.0) for h in range(classes)]
+    if filled > classes * bases:
+        masked.append(jnp.zeros((filled - classes * bases, basis.shape[1]), F32))
+    masked = jnp.concatenate(masked, axis=0)
+    masked_ref[...] = masked.astype(BF16)
+    turned_ref[...] = jnp.transpose(masked)
+    lane = lax.broadcasted_iota(jnp.int32, (1, filled), 1)
+    scales = jnp.ones((1, filled), F32)
+    for h in range(1, classes):
+        scales = jnp.where(lane >= h * bases, 1.0 / (2 * h + 1), scales)
+    line = lax.broadcasted_iota(jnp.int32, order_ref.shape, 0)
+    lane = lax.broadcasted_iota(jnp.int32, order_ref.shape, 1)
+    whose = jnp.zeros(order_ref.shape, jnp.int32)
+    for q in range(1, classes * groups):
+        whose = whose + (line >= q * unit).astype(jnp.int32)
+    inside = line - whose * unit
+    goal = whose * own + inside + jnp.where(inside >= own, filled - own, 0)
+    order_ref[...] = jnp.where((lane == goal) & (inside < 2 * own), 1.0, 0.0).astype(BF16)
 
     @pl.when(has_low)
     def _():
@@ -173,14 +243,18 @@
     def _():
         halo[1] = jnp.zeros(halo.shape[1:], BF16)
 
-    for i in range(reach):
-        fir(0, i, lambda q: x_ref[q] if q >= 0 else halo[0, reach + q])
-    last = (groups - 1) * block_rows
-    for i in range(block_rows - reach, block_rows):
-        fir(
-            groups - 1, i,
-            lambda q: x_ref[last + q] if q < block_rows else halo[1, q - block_rows],
-        )
+    @pl.loop(0, dates // 16)
+    def _(g):
+        taps = taps_of(g)
+        for part in range(2):
+            at, row = fir_rows(part, g)
+            low = [halo[0, q, at, :].astype(F32) for q in range(reach)]
+            low += [row(q) for q in range(2 * reach)]
+            high = [row(rows - 2 * reach + q) for q in range(2 * reach)]
+            high += [halo[1, q, at, :].astype(F32) for q in range(reach)]
+            for i in range(reach):
+                fir(i, at, taps, low[i : i + taps_count])
+                fir(rows - reach + i, at, taps, high[i : i + taps_count])
 
     def w_copy(o, src):
         return remote(
@@ -213,7 +287,9 @@
         w_copy(o, peers[o]).wait_recv()
 
     whole = what[...].reshape(2 * groups * dates, 2 * looks)
-    real, imag = project_gain(whole, weight_ref[0:1, 0:1], masked_ref[...], scales_ref[0:1, :], looks)
+    real, imag = project_gain(
+        whole, level_ref[...].astype(F32) / 16.0, masked_ref[...], turned_ref[...], scales, looks
+    )
     vsend[0] = real
     vsend[1] = imag
 
@@ -227,9 +303,6 @@
         v_copy(o, me).start()
     vrecv[me] = vsend[:, pl.ds(pl.multiple_of(me * dates, dates), dates), :]
 
-    zeros = jnp.zeros((SMOOTH_REACH,) + u.shape[1:], F32)
-    u[0:SMOOTH_REACH] = zeros
-    u[rows + SMOOTH_REACH : rows + 2 * SMOOTH_REACH] = zeros
     for o in range(groups):
         b = peers[o]
         if o:
@@ -251,7 +324,7 @@
         for h in range(classes):
             at = pl.ds(pl.multiple_of((h * groups + d) * unit, 8), unit)
             for j in range(-h, h + 1):
-                if place is None or 0 <= place + j < rows:
+                if 0 <= place + j < rows:
                     term = u[r + j + SMOOTH_REACH, at, :]
                     total = term if total is None else total + term
         return total
@@ -273,18 +346,36 @@
     def p_copy(o, src):
         return remote(psend.at[peers[o]], precv.at[src], s_p.at[o], r_p.at[src], peers[o], az)
 
+    def smooth_block(b, d, put):
+        first = b * block_rows
+        sums = [None] * block_rows
+        for h in range(classes):
+            at = pl.ds(pl.multiple_of((h * groups + d) * unit, 8), unit)
+            terms = [u[first + SMOOTH_REACH + j, at, :] for j in range(-h, block_rows + h)]
+            for i in range(block_rows):
+                for term in terms[i : i + 2 * h + 1]:
+                    sums[i] = term if sums[i] is None else sums[i] + term
+        for i in range(block_rows):
+            put(first + i, sums[i])
+
     for o in range(1, groups):
         d = peers[o]
 
-        @pl.loop(0, rows)
-        def _(r):
-            psend[d, r] = smooth(r, d, None).astype(BF16)
+        def put_sent(r, row, d=d):
+            psend[d, r] = row.astype(BF16)
+
+        @pl.loop(0, groups)
+        def _(b):
+            smooth_block(b, d, put_sent)
 
         p_copy(o, me).start()
 
-    @pl.loop(0, rows)
-    def _(r):
-        out_ref[r] = smooth(r, me, None)
+    def put_own(r, row):
+        out_ref[r] = row
+
+    @pl.loop(0, groups)
+    def _(b):
+        smooth_block(b, me, put_own)
 
     @pl.when(has_low)
     def _():
@@ -329,32 +420,21 @@
     unit = -(-2 * own // 8) * 8
     classes = SMOOTH_REACH + 1
 
-    x = slc_stack.transpose(2, 0, 1, 3).reshape(rows, parts * dates, cols)
-    taps = jnp.concatenate([fir_taps, fir_taps], axis=0)
-    chosen = look_index.reshape(1, looks)
-    chosen = jnp.broadcast_to(jnp.concatenate([chosen, chosen], axis=1), (8, 2 * looks))
-    weight = jnp.broadcast_to(shrink_level.astype(F32) / 16.0, (8, 128))
-    inside = window_half[None, :] == jnp.arange(classes)[:, None]
-    masked = jnp.where(inside[:, None, :], basis[None], jnp.zeros_like(basis)[None])
-    masked = masked.reshape(classes * bases, all_dates)
-    filled = -(-masked.shape[0] // 128) * 128
-    masked = jnp.pad(masked, ((0, filled - masked.shape[0]), (0, 0)))
-    scales = jnp.repeat(1.0 / (2.0 * jnp.arange(classes, dtype=F32) + 1.0), bases)
-    scales = jnp.broadcast_to(jnp.pad(scales, (0, filled - scales.shape[0])), (8, filled))
-    order_rows = np.zeros((classes, groups, unit, 2, filled), np.float32)
-    for h in range(classes):
-        for d in range(groups):
-            for part in range(2):
-                for k in range(own):
-                    order_rows[h, d, part * own + k, part, h * bases + d * own + k] = 1.0
-    order_rows = jnp.asarray(order_rows.reshape(classes * groups * unit, 2 * filled), BF16)
+    pitch = rows + 8
+    filled = -(-classes * bases // 128) * 128
 
     block_rows = rows // groups
     dma = pltpu.SemaphoreType.DMA
     vmem = pl.BlockSpec(memory_space=pltpu.VMEM)
     scratch = [
+        pltpu.VMEM((2 * dates * pitch, cols), F32),
         pltpu.VMEM((2, taps_count // 2, 2 * dates, cols), BF16),
+        pltpu.VMEM((2, taps_count // 2, 2 * dates, cols), BF16),
+        pltpu.VMEM((8, 2 * looks), jnp.int32),
         pltpu.VMEM((groups, 8, 2 * looks), jnp.int32),
+        pltpu.VMEM((filled, all_dates), BF16),
+        pltpu.VMEM((all_dates, filled), F32),
+        pltpu.VMEM((classes * groups * unit, 2 * filled), BF16),
         pltpu.VMEM((groups, 2 * dates, block_rows * cols), BF16),
         pltpu.VMEM((groups, 2, dates, 2 * looks), BF16),
         pltpu.VMEM((2, all_dates, 2 * looks), BF16),
@@ -373,15 +453,18 @@
         dma((2, groups)), dma((2, groups)),
     ]
     out = pl.pallas_call(
-        functools.partial(kernel, groups, slabs, looks, taps_count, unit),
+        functools.partial(kernel, groups, slabs, unit, own, pitch, filled),
         out_shape=jax.ShapeDtypeStruct((rows, unit, cols), F32),
-        in_specs=[vmem] * 7,
+        in_specs=[vmem] * 6,
         out_specs=vmem,
         scratch_shapes=scratch,
         compiler_params=pltpu.CompilerParams(
             collective_id=0, has_side_effects=True, vmem_limit_bytes=60 * 2**20
         ),
-    )(x, taps, chosen, weight, masked, scales, order_rows)
+    )(
+        slc_stack, fir_taps, look_index.reshape(1, looks), shrink_level,
+        window_half.reshape(1, all_dates), basis,
+    )
     out = out[:, : 2 * own].reshape(rows, 2, own, cols)
     return out.transpose(2, 1, 0, 3)
 

time: 48.2 us -> 40.6 us (0.84)
  local copies, waits for them, and re-layouts: 8.89 us -> 2.47 us
  Pallas kernels: 38.2 us -> 37.3 us
    transpose x1 -> x0, local copies, waits for them, and re-layouts: 2.6 us -> none  [on_device(): x = slc_stack.transpose(2, 0, 1, 3).reshape(rows, parts * dates, cols)]
    broadcast_in_dim x4 -> x0, local copies, waits for them, and re-layouts: 1.85 us -> none  [the longest x1 0.6 us: on_device(): jnp.broadcast_to(jnp.pad(scales, (0, filled - scales.shape[0])), (8, fill...]
    pallas_call x1, Pallas kernels: 38.2 us -> 37.3 us  [on_device(): pl.pallas_call(functools.partial(kernel, groups, slabs, unit, own, pitch,...]
    concatenate x1 -> x0, local copies, waits for them, and re-layouts: 0.74 us -> none  [on_device(): taps = jnp.concatenate([fir_taps, fir_taps], axis=0)]
    pad x2 -> x0, local copies, waits for them, and re-layouts: 0.63 us -> none  [the longest x1 0.63 us: on_device(): masked = jnp.pad(masked, ((0, filled - masked.shape[0]), (0, 0)))]
    unnamed x8 -> x3, local copies, waits for them, and re-layouts: 1.25 us -> 0.73 us
where the time goes in v2:
time: 40.6 us; the launch traced here: 40.4 us
  Pallas kernels  37.3 us (92%)
  local copies, waits for them, and re-layouts  2.47 us (6%)
  between operations  0.68 us (2%)
    pallas_call x1, Pallas kernels, on_device(): pl.pallas_call(functools.partial(kernel, groups, slabs, unit, own, pitch,...  37.3 us
    reshape x1, local copies, waits for them, and re-layouts, on_device(): out = out[:, :2 * own].reshape(rows, 2, own, cols)  1.74 us

profile of v2, /device:TPU:10, one launch (start us, length us, event | category | flops | bytes accessed | tf_op | source)
XLA Modules:
  0.0 40.4 jit_solution(6661588206174403358)
XLA Ops:
  0.0 0.0 copy-start
  0.7 0.0 copy-done
  0.7 0.7 %copy.7.taps_ref = f32[64,5]{1,0:T(8,128)} copy(f32[64,5]{0,1:T(8,128)S(1)} %copy-done) | data formatting | bytes 2560 | tf_op args[1]
  1.4 37.3 %shard_map.64 = f32[32,16,128]{2,1,0:T(8,128)} custom-call(bf16[2,64,32,128]{3,2,1,0:T(8,128)(2,1)} %x_ref.1, f32[64,5]{1,0:T(8,128)} %copy.7.taps_ref, s32[1,64]{1,0:T(1,128)} %bitcast.8, s32[1,1]{1,0:T(1,128)S(6)} %copy.11.level_ref, s32[1,256]{1,0:T(1,128)} %bitcast.7, bf16[32,256]{1,0:T(8,128)(2,1)} %basis_ref.1), custom_call_target="tpu_custom_call" | custom-call | tf_op jit(solution)/shard_map/pallas_call | solution.py:455
  38.7 1.7 %copy.10 = f32[32,2,8,128]{3,0,1,2:T(8,128)} copy(f32[32,2,8,128]{3,2,1,0:T(8,128)} %bitcast.6) | data formatting | bytes 524288 | tf_op jit(solution)/shard_map/reshape | solution.py:468
Async XLA Ops:
  0.0 0.7 %copy-start = (f32[64,5]{0,1:T(8,128)S(1)}, f32[64,5]{0,1:T(8,128)}, u32[]{:S(2)}) copy-start(f32[64,5]{0,1:T(8,128)} %param.7) | copy-start | bytes 3844

commit v3 on v2

--- a/solution.py
+++ b/solution.py
@@ -15,21 +15,43 @@
 BF16 = jnp.bfloat16
 
 
+def three_terms(array):
+    high = array.astype(BF16)
+    rest = array - high.astype(F32)
+    middle = rest.astype(BF16)
+    low = (rest - middle.astype(F32)).astype(BF16)
+    return high, middle, low
+
+
 def exact_dot(left, right):
-    return jnp.dot(left, right, precision=HIGHEST, preferred_element_type=F32)
+    l0, l1, l2 = three_terms(left)
+    r0, r1, r2 = three_terms(right)
+    width = right.shape[1]
+    small = jnp.dot(
+        jnp.concatenate([l0, l1], axis=1),
+        jnp.concatenate(
+            [jnp.concatenate([r1, r2], axis=1), jnp.concatenate([r0, r1], axis=1)], axis=0
+        ),
+        preferred_element_type=F32,
+    )
+    large = jnp.dot(
+        jnp.concatenate([l0, l2], axis=1), jnp.concatenate([r0, r0], axis=0),
+        preferred_element_type=F32,
+    )
+    return large + (small[:, :width] + small[:, width:])
 
 
 def split_dot(left, right):
-    high = right.astype(BF16)
-    low = (right - high.astype(F32)).astype(BF16)
+    high = left.astype(BF16)
+    low = (left - high.astype(F32)).astype(BF16)
     both = lax.dot_general(
-        left, jnp.concatenate([high, low], axis=0), (((1,), (1,)), ((), ())),
+        jnp.concatenate([high, low], axis=0), right, (((1,), (1,)), ((), ())),
         preferred_element_type=F32,
     )
-    return both[:, : right.shape[0]] + both[:, right.shape[0] :]
-
-
-def project_gain(what, weight, masked, turned, scales, looks):
+    return both[: left.shape[0]] + both[left.shape[0] :]
+
+
+def project_gain(top, what, weight, masked, spread, scales, looks):
     dates2, width = what.shape
     dates = dates2 // 2
     gram = lax.dot_general(what, what, (((0,), (0,)), ((), ())), preferred_element_type=F32)
@@ -83,19 +105,16 @@
             rho = rho * rho
     inner = full(scale * (f0 * eye + weight * mu * df + exact_dot(df, core)))
     base = weight * mu * scale * f0
-    seen = jnp.dot(masked, what[:dates], preferred_element_type=F32)
+    seen = jnp.dot(masked, top, preferred_element_type=F32)
     small = exact_dot(alpha * seen, inner)
-    both = split_dot(what, small)
-    real = (both[:dates] + base * turned) * scales
-    imag = both[dates:] * scales
-    return real.astype(BF16), imag.astype(BF16)
+    return (split_dot(small, what) + base * spread) * scales
 
 
 def kernel(
-    groups, slabs, unit, own, pitch, filled,
+    groups, slabs, unit, own, pitch,
     x_ref, taps_ref, look_ref, level_ref, window_ref, basis_ref, out_ref,
-    xf, halo_send, halo, idx_send, idx_all, masked_ref, turned_ref, order_ref,
-    z, wsend, what, vsend, vrecv, u, psend, precv, esend, erecv,
+    xf, halo_send, halo, idx_send, idx_all, masked_ref, spread_ref, order_ref,
+    z, wsend, what, vsend, vrecv, u, mine, psend, precv, esend, erecv,
     s_halo, r_halo, s_idx, r_idx, s_w, r_w, s_v, r_v, s_p, r_p, s_e, r_e,
 ):
     me = lax.axis_index("date")
@@ -209,22 +228,24 @@
     u[rows + SMOOTH_REACH : rows + 2 * SMOOTH_REACH] = zeros
     basis = basis_ref[...].astype(F32)
     masked = [jnp.where(window_ref[...] == h, basis, 0.0) for h in range(classes)]
-    if filled > classes * bases:
-        masked.append(jnp.zeros((filled - classes * bases, basis.shape[1]), F32))
     masked = jnp.concatenate(masked, axis=0)
     masked_ref[...] = masked.astype(BF16)
-    turned_ref[...] = jnp.transpose(masked)
-    lane = lax.broadcasted_iota(jnp.int32, (1, filled), 1)
-    scales = jnp.ones((1, filled), F32)
+    spread = []
+    for d in range(groups):
+        part = masked[:, d * dates : (d + 1) * dates]
+        spread += [part, jnp.zeros_like(part)]
+    spread_ref[...] = jnp.concatenate(spread, axis=1)
+    line = lax.broadcasted_iota(jnp.int32, (classes * bases, 1), 0)
+    scales = jnp.ones((classes * bases, 1), F32)
     for h in range(1, classes):
-        scales = jnp.where(lane >= h * bases, 1.0 / (2 * h + 1), scales)
+        scales = jnp.where(line >= h * bases, 1.0 / (2 * h + 1), scales)
     line = lax.broadcasted_iota(jnp.int32, order_ref.shape, 0)
     lane = lax.broadcasted_iota(jnp.int32, order_ref.shape, 1)
     whose = jnp.zeros(order_ref.shape, jnp.int32)
     for q in range(1, classes * groups):
         whose = whose + (line >= q * unit).astype(jnp.int32)
     inside = line - whose * unit
-    goal = whose * own + inside + jnp.where(inside >= own, filled - own, 0)
+    goal = whose * own + (inside >> 1) + (inside & 1) * (classes * bases)
     order_ref[...] = jnp.where((lane == goal) & (inside < 2 * own), 1.0, 0.0).astype(BF16)
 
     @pl.when(has_low)
@@ -258,8 +279,7 @@
 
     def w_copy(o, src):
         return remote(
-            wsend.at[peers[o]],
-            what.at[:, pl.ds(pl.multiple_of(src * dates, dates), dates), :],
+            wsend.at[peers[o]], what.at[src],
             s_w.at[o], r_w.at[src], peers[o], az,
         )
 
@@ -272,48 +292,44 @@
         pick = (pixel == chosen).astype(F32).astype(BF16)
         sample = jnp.dot(z[b], pick, preferred_element_type=F32)
         left = lax.broadcasted_iota(jnp.int32, (dates, 2 * looks), 1) < looks
-        real, imag = sample[:dates], sample[dates:]
-        top = jnp.where(left, real, -imag).astype(BF16)
-        bottom = jnp.where(left, imag, real).astype(BF16)
+        sample = jnp.where(left, sample[:dates], sample[dates:]).astype(BF16)
         if o:
-            wsend[b, 0] = top
-            wsend[b, 1] = bottom
+            wsend[b] = sample
             w_copy(o, me).start()
         else:
-            own = pl.ds(pl.multiple_of(me * dates, dates), dates)
-            what[0, own, :] = top
-            what[1, own, :] = bottom
+            what[me] = sample
     for o in range(1, groups):
         w_copy(o, peers[o]).wait_recv()
 
-    whole = what[...].reshape(2 * groups * dates, 2 * looks)
-    real, imag = project_gain(
-        whole, level_ref[...].astype(F32) / 16.0, masked_ref[...], turned_ref[...], scales, looks
-    )
-    vsend[0] = real
-    vsend[1] = imag
+    tops = []
+    both = []
+    for d in range(groups):
+        sample = what[d].astype(F32)
+        top = jnp.where(left, sample, -sample).astype(BF16)
+        tops.append(top)
+        both += [top, pltpu.roll(sample, looks, 1).astype(BF16)]
+    found = project_gain(
+        jnp.concatenate(tops, axis=0), jnp.concatenate(both, axis=0),
+        level_ref[...].astype(F32) / 16.0, masked_ref[...], spread_ref[...], scales, looks,
+    ).astype(BF16)
+    for d in range(groups):
+        vsend[d] = found[:, d * 2 * dates : (d + 1) * 2 * dates]
 
     def v_copy(o, src):
-        return remote(
-            vsend.at[:, pl.ds(pl.multiple_of(peers[o] * dates, dates), dates), :],
-            vrecv.at[src], s_v.at[o], r_v.at[src], peers[o], az,
-        )
+        return remote(vsend.at[peers[o]], vrecv.at[src], s_v.at[o], r_v.at[src], peers[o], az)
 
     for o in range(1, groups):
         v_copy(o, me).start()
-    vrecv[me] = vsend[:, pl.ds(pl.multiple_of(me * dates, dates), dates), :]
+    vrecv[me] = vsend[me]
 
     for o in range(groups):
         b = peers[o]
         if o:
             v_copy(o, b).wait_recv()
-        v_re = vrecv[b, 0]
-        v_im = vrecv[b, 1]
-        upper = jnp.concatenate([v_re, v_im], axis=0)
-        lower = jnp.concatenate([-v_im, v_re], axis=0)
-        mix = lax.dot_general(
-            order_ref[...], jnp.concatenate([upper, lower], axis=1),
-            (((1,), (1,)), ((), ())), preferred_element_type=F32,
+        upper = vrecv[b]
+        lower = jnp.concatenate([-upper[:, dates:], upper[:, :dates]], axis=1)
+        mix = jnp.dot(
+            order_ref[...], jnp.concatenate([upper, lower], axis=0), preferred_element_type=F32
         ).astype(BF16)
         found = jnp.dot(mix, z[b], preferred_element_type=F32)
         for i in range(block_rows):
@@ -371,7 +387,7 @@
         p_copy(o, me).start()
 
     def put_own(r, row):
-        out_ref[r] = row
+        mine[r] = row
 
     @pl.loop(0, groups)
     def _(b):
@@ -383,7 +399,7 @@
             e_copy(1, o, peers[o], az - 1).wait_recv()
         for i in range(SMOOTH_REACH):
             for o in range(groups):
-                out_ref[i] += erecv[0, peers[o], i].astype(F32)
+                mine[i] += erecv[0, peers[o], i].astype(F32)
 
     @pl.when(has_high)
     def _():
@@ -391,11 +407,19 @@
             e_copy(0, o, peers[o], az + 1).wait_recv()
         for i in range(SMOOTH_REACH):
             for o in range(groups):
-                out_ref[rows - SMOOTH_REACH + i] += erecv[1, peers[o], i].astype(F32)
+                mine[rows - SMOOTH_REACH + i] += erecv[1, peers[o], i].astype(F32)
 
     for o in range(1, groups):
         p_copy(o, peers[o]).wait_recv()
-        out_ref[...] += precv[peers[o]].astype(F32)
+        if o < groups - 1:
+            mine[...] += precv[peers[o]].astype(F32)
+
+    @pl.loop(0, groups)
+    def _(b):
+        for i in range(block_rows):
+            r = b * block_rows + i
+            row = mine[r] + precv[peers[groups - 1], r].astype(F32)
+            out_ref[pl.ds(r, 2 * own, stride=rows), :] = row[: 2 * own]
 
     pl.when(has_low)(lambda: halo_down().wait_send())
     pl.when(has_high)(lambda: halo_up().wait_send())
@@ -421,7 +445,6 @@
     classes = SMOOTH_REACH + 1
 
     pitch = rows + 8
-    filled = -(-classes * bases // 128) * 128
 
     block_rows = rows // groups
     dma = pltpu.SemaphoreType.DMA
@@ -432,15 +455,16 @@
         pltpu.VMEM((2, taps_count // 2, 2 * dates, cols), BF16),
         pltpu.VMEM((8, 2 * looks), jnp.int32),
         pltpu.VMEM((groups, 8, 2 * looks), jnp.int32),
-        pltpu.VMEM((filled, all_dates), BF16),
-        pltpu.VMEM((all_dates, filled), F32),
-        pltpu.VMEM((classes * groups * unit, 2 * filled), BF16),
+        pltpu.VMEM((classes * bases, all_dates), BF16),
+        pltpu.VMEM((classes * bases, 2 * all_dates), F32),
+        pltpu.VMEM((classes * groups * unit, 2 * classes * bases), BF16),
         pltpu.VMEM((groups, 2 * dates, block_rows * cols), BF16),
-        pltpu.VMEM((groups, 2, dates, 2 * looks), BF16),
-        pltpu.VMEM((2, all_dates, 2 * looks), BF16),
-        pltpu.VMEM((2, all_dates, filled), BF16),
-        pltpu.VMEM((groups, 2, dates, filled), BF16),
+        pltpu.VMEM((groups, dates, 2 * looks), BF16),
+        pltpu.VMEM((groups, dates, 2 * looks), BF16),
+        pltpu.VMEM((groups, classes * bases, 2 * dates), BF16),
+        pltpu.VMEM((groups, classes * bases, 2 * dates), BF16),
         pltpu.VMEM((rows + 2 * SMOOTH_REACH, classes * groups * unit, cols), F32),
+        pltpu.VMEM((rows, unit, cols), F32),
         pltpu.VMEM((groups, rows, unit, cols), BF16),
         pltpu.VMEM((groups, rows, unit, cols), BF16),
         pltpu.VMEM((2, groups, SMOOTH_REACH, unit, cols), BF16),
@@ -453,8 +477,8 @@
         dma((2, groups)), dma((2, groups)),
     ]
     out = pl.pallas_call(
-        functools.partial(kernel, groups, slabs, unit, own, pitch, filled),
-        out_shape=jax.ShapeDtypeStruct((rows, unit, cols), F32),
+        functools.partial(kernel, groups, slabs, unit, own, pitch),
+        out_shape=jax.ShapeDtypeStruct((2 * own * rows, cols), F32),
         in_specs=[vmem] * 6,
         out_specs=vmem,
         scratch_shapes=scratch,
@@ -465,8 +489,7 @@
         slc_stack, fir_taps, look_index.reshape(1, looks), shrink_level,
         window_half.reshape(1, all_dates), basis,
     )
-    out = out[:, : 2 * own].reshape(rows, 2, own, cols)
-    return out.transpose(2, 1, 0, 3)
+    return out.reshape(own, 2, rows, cols)
 
 
 def solution(mesh):

time: 40.6 us -> 38.7 us (0.953)
  the two profiles are of different devices: /device:TPU:10 before, /device:TPU:11 now
where the time goes in v3:
time: 38.7 us; the launch traced here: 38.5 us
  Pallas kernels  35.4 us (91%)
  local copies, waits for them, and re-layouts  2.4 us (6%)
  between operations  0.68 us (2%)
    pallas_call x1, Pallas kernels, on_device(): pl.pallas_call(functools.partial(kernel, groups, slabs, unit, own, pitch)...  35.4 us
    unnamed x4, local copies, waits for them, and re-layouts  2.4 us

profile of v3, /device:TPU:11, one launch (start us, length us, event | category | flops | bytes accessed | tf_op | source)
XLA Modules:
  0.0 38.5 jit_solution(17088759199505388657)
XLA Ops:
  0.0 0.0 copy-start
  0.7 0.0 copy-done
  0.7 0.7 %copy.7.taps_ref = f32[64,5]{1,0:T(8,128)} copy(f32[64,5]{0,1:T(8,128)S(1)} %copy-done) | data formatting | bytes 2560 | tf_op args[1]
  1.4 35.4 %shard_map.64 = f32[512,128]{1,0:T(8,128)} custom-call(bf16[2,64,32,128]{3,2,1,0:T(8,128)(2,1)} %x_ref.1, f32[64,5]{1,0:T(8,128)} %copy.7.taps_ref, s32[1,64]{1,0:T(1,128)} %bitcast.5, s32[1,1]{1,0:T(1,128)S(6)} %copy.9.level_ref, s32[1,256]{1,0:T(1,128)} %bitcast.4, bf16[32,256]{1,0:T(8,128)(2,1)} %basis_ref.1), custom_call_target="tpu_custom_call" | custom-call | tf_op jit(solution)/shard_map/pallas_call | solution.py:479
  36.8 1.7 %copy.10 = f32[8,2,32,128]{3,2,1,0:T(8,128)} copy(f32[8,2,32,128]{3,2,1,0:T(8,128)} %bitcast.3) | data formatting | bytes 524288
Async XLA Ops:
  0.0 0.7 %copy-start = (f32[64,5]{0,1:T(8,128)S(1)}, f32[64,5]{0,1:T(8,128)}, u32[]{:S(2)}) copy-start(f32[64,5]{0,1:T(8,128)} %param.7) | copy-start | bytes 3844

commit v4 on v3

--- a/solution.py
+++ b/solution.py
@@ -322,10 +322,11 @@
         v_copy(o, me).start()
     vrecv[me] = vsend[me]
 
-    for o in range(groups):
-        b = peers[o]
-        if o:
-            v_copy(o, b).wait_recv()
+    def mix_block(b):
+        @pl.when(me != b)
+        def _():
+            v_copy(1, b).wait_recv()
+
         upper = vrecv[b]
         lower = jnp.concatenate([-upper[:, dates:], upper[:, :dates]], axis=1)
         mix = jnp.dot(
@@ -345,22 +346,15 @@
                     total = term if total is None else total + term
         return total
 
-    def e_copy(side, o, src, target):
+    half = groups // 2
+    half_rows = half * block_rows
+
+    def p_copy(o, src, part):
+        at = pl.ds(part * half_rows, half_rows)
         return remote(
-            esend.at[side, peers[o]], erecv.at[1 - side, src],
-            s_e.at[side, o], r_e.at[1 - side, src], peers[o], target,
+            psend.at[peers[o], at], precv.at[src, at],
+            s_p.at[part, o], r_p.at[part, src], peers[o], az,
         )
-
-    for o in range(groups):
-        d = peers[o]
-        for i in range(SMOOTH_REACH):
-            esend[0, d, i] = smooth(i - SMOOTH_REACH, d, i - SMOOTH_REACH).astype(BF16)
-            esend[1, d, i] = smooth(rows + i, d, rows + i).astype(BF16)
-        pl.when(has_low)(lambda o=o: e_copy(0, o, me, az - 1).start())
-        pl.when(has_high)(lambda o=o: e_copy(1, o, me, az + 1).start())
-
-    def p_copy(o, src):
-        return remote(psend.at[peers[o]], precv.at[src], s_p.at[o], r_p.at[src], peers[o], az)
 
     def smooth_block(b, d, put):
         first = b * block_rows
@@ -374,17 +368,34 @@
         for i in range(block_rows):
             put(first + i, sums[i])
 
-    for o in range(1, groups):
+    for part in range(2):
+        for b in range(half + 1) if part == 0 else range(half + 1, groups):
+            mix_block(b)
+        for o in range(1, groups):
+            d = peers[o]
+
+            def put_sent(r, row, d=d):
+                psend[d, r] = row.astype(BF16)
+
+            @pl.loop(part * half, (part + 1) * half)
+            def _(b):
+                smooth_block(b, d, put_sent)
+
+            p_copy(o, me, part).start()
+
+    def e_copy(side, o, src, target):
+        return remote(
+            esend.at[side, peers[o]], erecv.at[1 - side, src],
+            s_e.at[side, o], r_e.at[1 - side, src], peers[o], target,
+        )
+
+    for o in range(groups):
         d = peers[o]
-
-        def put_sent(r, row, d=d):
-            psend[d, r] = row.astype(BF16)
-
-        @pl.loop(0, groups)
-        def _(b):
-            smooth_block(b, d, put_sent)
-
-        p_copy(o, me).start()
+        for i in range(SMOOTH_REACH):
+            esend[0, d, i] = smooth(i - SMOOTH_REACH, d, i - SMOOTH_REACH).astype(BF16)
+            esend[1, d, i] = smooth(rows + i, d, rows + i).astype(BF16)
+        pl.when(has_low)(lambda o=o: e_copy(0, o, me, az - 1).start())
+        pl.when(has_high)(lambda o=o: e_copy(1, o, me, az + 1).start())
 
     def put_own(r, row):
         mine[r] = row
@@ -410,7 +421,8 @@
                 mine[rows - SMOOTH_REACH + i] += erecv[1, peers[o], i].astype(F32)
 
     for o in range(1, groups):
-        p_copy(o, peers[o]).wait_recv()
+        for part in range(2):
+            p_copy(o, peers[o], part).wait_recv()
         if o < groups - 1:
             mine[...] += precv[peers[o]].astype(F32)
 
@@ -428,7 +440,8 @@
             idx_copy(o, me).wait_send()
             w_copy(o, me).wait_send()
             v_copy(o, me).wait_send()
-            p_copy(o, me).wait_send()
+            for part in range(2):
+                p_copy(o, me, part).wait_send()
         pl.when(has_low)(lambda o=o: e_copy(0, o, me, az - 1).wait_send())
         pl.when(has_high)(lambda o=o: e_copy(1, o, me, az + 1).wait_send())
 
@@ -473,7 +486,7 @@
         dma((groups,)), dma((groups,)),
         dma((groups,)), dma((groups,)),
         dma((groups,)), dma((groups,)),
-        dma((groups,)), dma((groups,)),
+        dma((2, groups)), dma((2, groups)),
         dma((2, groups)), dma((2, groups)),
     ]
     out = pl.pallas_call(

time: 38.7 us -> 40.2 us (1.039)
  the two profiles are of different devices: /device:TPU:11 before, /device:TPU:1 now
where the time goes in v4:
time: 40.2 us; the launch traced here: 40 us
  Pallas kernels  37 us (92%)
  local copies, waits for them, and re-layouts  2.4 us (6%)
  between operations  0.68 us (2%)
    pallas_call x1, Pallas kernels, on_device(): pl.pallas_call(functools.partial(kernel, groups, slabs, unit, own, pitch)...  37 us
    unnamed x4, local copies, waits for them, and re-layouts  2.4 us

profile of v4, /device:TPU:1, one launch (start us, length us, event | category | flops | bytes accessed | tf_op | source)
XLA Modules:
  0.0 40.0 jit_solution(2620368830328558929)
XLA Ops:
  0.0 0.0 copy-start
  0.7 0.0 copy-done
  0.7 0.7 %copy.7.taps_ref = f32[64,5]{1,0:T(8,128)} copy(f32[64,5]{0,1:T(8,128)S(1)} %copy-done) | data formatting | bytes 2560 | tf_op args[1]
  1.4 37.0 %shard_map.64 = f32[512,128]{1,0:T(8,128)} custom-call(bf16[2,64,32,128]{3,2,1,0:T(8,128)(2,1)} %x_ref.1, f32[64,5]{1,0:T(8,128)} %copy.7.taps_ref, s32[1,64]{1,0:T(1,128)} %bitcast.5, s32[1,1]{1,0:T(1,128)S(6)} %copy.9.level_ref, s32[1,256]{1,0:T(1,128)} %bitcast.4, bf16[32,256]{1,0:T(8,128)(2,1)} %basis_ref.1), custom_call_target="tpu_custom_call" | custom-call | tf_op jit(solution)/shard_map/pallas_call | solution.py:492
  38.4 1.7 %copy.10 = f32[8,2,32,128]{3,2,1,0:T(8,128)} copy(f32[8,2,32,128]{3,2,1,0:T(8,128)} %bitcast.3) | data formatting | bytes 524288
Async XLA Ops:
  0.0 0.7 %copy-start = (f32[64,5]{0,1:T(8,128)S(1)}, f32[64,5]{0,1:T(8,128)}, u32[]{:S(2)}) copy-start(f32[64,5]{0,1:T(8,128)} %param.7) | copy-start | bytes 3844

commit v5 on v3

--- a/solution.py
+++ b/solution.py
@@ -140,13 +140,11 @@
 
     @pl.when(has_low)
     def _():
-        for o in range(groups):
-            greet(peers[o], az - 1)
+        greet(me, az - 1)
 
     @pl.when(has_high)
     def _():
-        for o in range(groups):
-            greet(peers[o], az + 1)
+        greet(me, az + 1)
 
     chosen = jnp.broadcast_to(look_ref[...], (8, looks))
     idx_send[...] = jnp.concatenate([chosen, chosen], axis=1)
@@ -178,7 +176,7 @@
 
     pl.semaphore_wait(
         barrier,
-        groups - 1 + groups * (has_low.astype(jnp.int32) + has_high.astype(jnp.int32)),
+        groups - 1 + has_low.astype(jnp.int32) + has_high.astype(jnp.int32),
     )
 
     def remote(src, dst, send, recv, d, a):
@@ -322,10 +320,11 @@
         v_copy(o, me).start()
     vrecv[me] = vsend[me]
 
-    for o in range(groups):
-        b = peers[o]
-        if o:
-            v_copy(o, b).wait_recv()
+    def mix_block(b):
+        @pl.when(me != b)
+        def _():
+            v_copy(1, b).wait_recv()
+
         upper = vrecv[b]
         lower = jnp.concatenate([-upper[:, dates:], upper[:, :dates]], axis=1)
         mix = jnp.dot(
@@ -335,32 +334,42 @@
         for i in range(block_rows):
             u[SMOOTH_REACH + b * block_rows + i] = found[:, i * cols : (i + 1) * cols]
 
-    def smooth(r, d, place):
+    def smooth(r):
         total = None
         for h in range(classes):
-            at = pl.ds(pl.multiple_of((h * groups + d) * unit, 8), unit)
-            for j in range(-h, h + 1):
-                if 0 <= place + j < rows:
-                    term = u[r + j + SMOOTH_REACH, at, :]
-                    total = term if total is None else total + term
-        return total
-
-    def e_copy(side, o, src, target):
+            at = slice(h * groups * unit, (h + 1) * groups * unit)
+            for j in range(max(r - h, 0), min(r + h, rows - 1) + 1):
+                term = u[j + SMOOTH_REACH, at, :]
+                total = term if total is None else total + term
+        return total.reshape(groups, unit, cols).astype(BF16)
+
+    def e_copy(side, target):
         return remote(
-            esend.at[side, peers[o]], erecv.at[1 - side, src],
-            s_e.at[side, o], r_e.at[1 - side, src], peers[o], target,
+            esend.at[side], erecv.at[1 - side], s_e.at[side], r_e.at[1 - side], me, target
         )
 
-    for o in range(groups):
-        d = peers[o]
-        for i in range(SMOOTH_REACH):
-            esend[0, d, i] = smooth(i - SMOOTH_REACH, d, i - SMOOTH_REACH).astype(BF16)
-            esend[1, d, i] = smooth(rows + i, d, rows + i).astype(BF16)
-        pl.when(has_low)(lambda o=o: e_copy(0, o, me, az - 1).start())
-        pl.when(has_high)(lambda o=o: e_copy(1, o, me, az + 1).start())
-
-    def p_copy(o, src):
-        return remote(psend.at[peers[o]], precv.at[src], s_p.at[o], r_p.at[src], peers[o], az)
+    mix_block(0)
+    for i in range(SMOOTH_REACH):
+        esend[0, i] = smooth(i - SMOOTH_REACH)
+    pl.when(has_low)(lambda: e_copy(0, az - 1).start())
+    mix_block(groups - 1)
+    for i in range(SMOOTH_REACH):
+        esend[1, i] = smooth(rows + i)
+    pl.when(has_high)(lambda: e_copy(1, az + 1).start())
+    for b in range(1, groups - 1):
+        mix_block(b)
+
+    chunks = (
+        pl.ds(block_rows, rows - 2 * block_rows),
+        pl.ds(0, block_rows),
+        pl.ds(rows - block_rows, block_rows),
+    )
+
+    def p_copy(o, src, chunk):
+        return remote(
+            psend.at[peers[o], chunks[chunk]], precv.at[src, chunks[chunk]],
+            s_p.at[chunk, o], r_p.at[chunk, src], peers[o], az,
+        )
 
     def smooth_block(b, d, put):
         first = b * block_rows
@@ -374,51 +383,72 @@
         for i in range(block_rows):
             put(first + i, sums[i])
 
-    for o in range(1, groups):
-        d = peers[o]
-
-        def put_sent(r, row, d=d):
+    def put_sent(d):
+        def put(r, row):
             psend[d, r] = row.astype(BF16)
 
-        @pl.loop(0, groups)
-        def _(b):
-            smooth_block(b, d, put_sent)
-
-        p_copy(o, me).start()
+        return put
 
     def put_own(r, row):
         mine[r] = row
 
-    @pl.loop(0, groups)
+    def edge_block(side, d, put):
+        first = side * (rows - SMOOTH_REACH)
+
+        def put_edge(r, row):
+            if first <= r < first + SMOOTH_REACH:
+                row = row + erecv[side, r - first, d].astype(F32)
+            put(r, row)
+
+        smooth_block(side * (groups - 1), d, put_edge)
+
+    for o in range(1, groups):
+
+        @pl.loop(1, groups - 1)
+        def _(b, o=o):
+            smooth_block(b, peers[o], put_sent(peers[o]))
+
+        p_copy(o, me, 0).start()
+
+    @pl.when(has_low)
+    def _():
+        e_copy(1, az - 1).wait_recv()
+
+    @pl.when(jnp.logical_not(has_low))
+    def _():
+        erecv[0] = jnp.zeros(erecv.shape[1:], BF16)
+
+    @pl.when(has_high)
+    def _():
+        e_copy(0, az + 1).wait_recv()
+
+    @pl.when(jnp.logical_not(has_high))
+    def _():
+        erecv[1] = jnp.zeros(erecv.shape[1:], BF16)
+
+    for o in range(1, groups):
+        for side in range(2):
+            edge_block(side, peers[o], put_sent(peers[o]))
+            p_copy(o, me, 1 + side).start()
+
+    @pl.loop(1, groups - 1)
     def _(b):
         smooth_block(b, me, put_own)
 
-    @pl.when(has_low)
-    def _():
-        for o in range(groups):
-            e_copy(1, o, peers[o], az - 1).wait_recv()
-        for i in range(SMOOTH_REACH):
-            for o in range(groups):
-                mine[i] += erecv[0, peers[o], i].astype(F32)
-
-    @pl.when(has_high)
-    def _():
-        for o in range(groups):
-            e_copy(0, o, peers[o], az + 1).wait_recv()
-        for i in range(SMOOTH_REACH):
-            for o in range(groups):
-                mine[rows - SMOOTH_REACH + i] += erecv[1, peers[o], i].astype(F32)
-
-    for o in range(1, groups):
-        p_copy(o, peers[o]).wait_recv()
-        if o < groups - 1:
-            mine[...] += precv[peers[o]].astype(F32)
+    for side in range(2):
+        edge_block(side, me, put_own)
+
+    for chunk in range(3):
+        for o in range(1, groups):
+            p_copy(o, peers[o], chunk).wait_recv()
 
     @pl.loop(0, groups)
     def _(b):
         for i in range(block_rows):
             r = b * block_rows + i
-            row = mine[r] + precv[peers[groups - 1], r].astype(F32)
+            row = mine[r]
+            for o in range(1, groups):
+                row = row + precv[peers[o], r].astype(F32)
             out_ref[pl.ds(r, 2 * own, stride=rows), :] = row[: 2 * own]
 
     pl.when(has_low)(lambda: halo_down().wait_send())
@@ -428,9 +458,10 @@
             idx_copy(o, me).wait_send()
             w_copy(o, me).wait_send()
             v_copy(o, me).wait_send()
-            p_copy(o, me).wait_send()
-        pl.when(has_low)(lambda o=o: e_copy(0, o, me, az - 1).wait_send())
-        pl.when(has_high)(lambda o=o: e_copy(1, o, me, az + 1).wait_send())
+            for chunk in range(3):
+                p_copy(o, me, chunk).wait_send()
+    pl.when(has_low)(lambda: e_copy(0, az - 1).wait_send())
+    pl.when(has_high)(lambda: e_copy(1, az + 1).wait_send())
 
 
 def on_device(slc_stack, fir_taps, look_index, shrink_level, window_half, basis):
@@ -467,14 +498,14 @@
         pltpu.VMEM((rows, unit, cols), F32),
         pltpu.VMEM((groups, rows, unit, cols), BF16),
         pltpu.VMEM((groups, rows, unit, cols), BF16),
-        pltpu.VMEM((2, groups, SMOOTH_REACH, unit, cols), BF16),
-        pltpu.VMEM((2, groups, SMOOTH_REACH, unit, cols), BF16),
+        pltpu.VMEM((2, SMOOTH_REACH, groups, unit, cols), BF16),
+        pltpu.VMEM((2, SMOOTH_REACH, groups, unit, cols), BF16),
         dma((2,)), dma((2,)),
         dma((groups,)), dma((groups,)),
         dma((groups,)), dma((groups,)),
         dma((groups,)), dma((groups,)),
-        dma((groups,)), dma((groups,)),
-        dma((2, groups)), dma((2, groups)),
+        dma((3, groups)), dma((3, groups)),
+        dma((2,)), dma((2,)),
     ]
     out = pl.pallas_call(
         functools.partial(kernel, groups, slabs, unit, own, pitch),

time: 38.7 us -> 38.3 us (0.990)
  the two profiles are of different devices: /device:TPU:11 before, /device:TPU:0 now
where the time goes in v5:
time: 38.3 us; the launch traced here: 38.1 us
  Pallas kernels  35 us (91%)
  local copies, waits for them, and re-layouts  2.4 us (6%)
  between operations  0.68 us (2%)
    pallas_call x1, Pallas kernels, on_device(): pl.pallas_call(functools.partial(kernel, groups, slabs, unit, own, pitch)...  35 us
    unnamed x4, local copies, waits for them, and re-layouts  2.4 us

profile of v5, /device:TPU:0, one launch (start us, length us, event | category | flops | bytes accessed | tf_op | source)
XLA Modules:
  0.0 38.1 jit_solution(8751845436047147321)
XLA Ops:
  0.0 0.0 copy-start
  0.7 0.0 copy-done
  0.7 0.7 %copy.7.taps_ref = f32[64,5]{1,0:T(8,128)} copy(f32[64,5]{0,1:T(8,128)S(1)} %copy-done) | data formatting | bytes 2560 | tf_op args[1]
  1.4 35.0 %shard_map.64 = f32[512,128]{1,0:T(8,128)} custom-call(bf16[2,64,32,128]{3,2,1,0:T(8,128)(2,1)} %x_ref.1, f32[64,5]{1,0:T(8,128)} %copy.7.taps_ref, s32[1,64]{1,0:T(1,128)} %bitcast.5, s32[1,1]{1,0:T(1,128)S(6)} %copy.9.level_ref, s32[1,256]{1,0:T(1,128)} %bitcast.4, bf16[32,256]{1,0:T(8,128)(2,1)} %basis_ref.1), custom_call_target="tpu_custom_call" | custom-call | tf_op jit(solution)/shard_map/pallas_call | solution.py:510
  36.4 1.7 %copy.10 = f32[8,2,32,128]{3,2,1,0:T(8,128)} copy(f32[8,2,32,128]{3,2,1,0:T(8,128)} %bitcast.3) | data formatting | bytes 524288
Async XLA Ops:
  0.0 0.7 %copy-start = (f32[64,5]{0,1:T(8,128)S(1)}, f32[64,5]{0,1:T(8,128)}, u32[]{:S(2)}) copy-start(f32[64,5]{0,1:T(8,128)} %param.7) | copy-start | bytes 3844

commit v6 on v5

--- a/solution.py
+++ b/solution.py
@@ -113,14 +113,14 @@
 def kernel(
     groups, slabs, unit, own, pitch,
     x_ref, taps_ref, look_ref, level_ref, window_ref, basis_ref, out_ref,
-    xf, halo_send, halo, idx_send, idx_all, masked_ref, spread_ref, order_ref,
+    xf, taps_wide, halo_send, halo, idx_send, idx_all, masked_ref, spread_ref, order_ref,
     z, wsend, what, vsend, vrecv, u, mine, psend, precv, esend, erecv,
     s_halo, r_halo, s_idx, r_idx, s_w, r_w, s_v, r_v, s_p, r_p, s_e, r_e,
 ):
     me = lax.axis_index("date")
     az = lax.axis_index("az")
     _, dates, rows, cols = x_ref.shape
-    taps_count = taps_ref.shape[1]
+    taps_count = taps_ref.shape[0]
     looks = look_ref.shape[1]
     bases = basis_ref.shape[0]
     block_rows = rows // groups
@@ -200,9 +200,15 @@
         idx_copy(o, me).start()
     idx_all[me] = idx_send[...]
 
+    line = lax.broadcasted_iota(jnp.int32, (dates, dates), 0)
+    column = lax.broadcasted_iota(jnp.int32, (dates, dates), 1)
+    for j in range(taps_count):
+        own_tap = jnp.where(line == column, taps_ref[j : j + 1, :], 0.0)
+        taps_wide[j] = jnp.broadcast_to(jnp.sum(own_tap, axis=1, keepdims=True), (dates, cols))
+
     def taps_of(g):
-        taps = taps_ref[pl.ds(pl.multiple_of(g * 16, 16), 16), :]
-        return [jnp.broadcast_to(taps[:, j : j + 1], (16, cols)) for j in range(taps_count)]
+        at = pl.ds(pl.multiple_of(g * 16, 16), 16)
+        return [taps_wide[j, at, :] for j in range(taps_count)]
 
     def fir(r, at, taps, window):
         total = taps[0] * window[0]
@@ -220,6 +226,64 @@
             for r in range(reach, rows - reach):
                 window = window[-2 * reach :] + [row(r + reach)]
                 fir(r, at, taps, window)
+
+    left = lax.broadcasted_iota(jnp.int32, (dates, 2 * looks), 1) < looks
+
+    def w_copy(b, src):
+        return remote(wsend.at[b], what.at[src], s_w.at[b], r_w.at[src], b, az)
+
+    def send_looks(b):
+        @pl.when(me != b)
+        def _():
+            idx_copy(1, b).wait_recv()
+
+        pixel = lax.broadcasted_iota(jnp.int32, (block_rows * cols, 2 * looks), 0)
+        pick = (pixel == idx_all[b][0:1, :]).astype(F32).astype(BF16)
+        sample = jnp.dot(z[b], pick, preferred_element_type=F32)
+        wsend[b] = jnp.where(left, sample[:dates], sample[dates:]).astype(BF16)
+
+        @pl.when(me != b)
+        def _():
+            w_copy(b, me).start()
+
+        @pl.when(me == b)
+        def _():
+            what[b] = wsend[b]
+
+    for b in range(1, groups - 1):
+        send_looks(b)
+
+    @pl.when(has_low)
+    def _():
+        halo_up().wait_recv()
+
+    @pl.when(jnp.logical_not(has_low))
+    def _():
+        halo[0] = jnp.zeros(halo.shape[1:], BF16)
+
+    @pl.when(has_high)
+    def _():
+        halo_down().wait_recv()
+
+    @pl.when(jnp.logical_not(has_high))
+    def _():
+        halo[1] = jnp.zeros(halo.shape[1:], BF16)
+
+    @pl.loop(0, dates // 16)
+    def _(g):
+        taps = taps_of(g)
+        for part in range(2):
+            at, row = fir_rows(part, g)
+            low = [halo[0, q, at, :].astype(F32) for q in range(reach)]
+            low += [row(q) for q in range(2 * reach)]
+            high = [row(rows - 2 * reach + q) for q in range(2 * reach)]
+            high += [halo[1, q, at, :].astype(F32) for q in range(reach)]
+            for i in range(reach):
+                fir(i, at, taps, low[i : i + taps_count])
+                fir(rows - reach + i, at, taps, high[i : i + taps_count])
+
+    send_looks(0)
+    send_looks(groups - 1)
 
     zeros = jnp.zeros((SMOOTH_REACH,) + u.shape[1:], F32)
     u[0:SMOOTH_REACH] = zeros
@@ -246,58 +310,8 @@
     goal = whose * own + (inside >> 1) + (inside & 1) * (classes * bases)
     order_ref[...] = jnp.where((lane == goal) & (inside < 2 * own), 1.0, 0.0).astype(BF16)
 
-    @pl.when(has_low)
-    def _():
-        halo_up().wait_recv()
-
-    @pl.when(jnp.logical_not(has_low))
-    def _():
-        halo[0] = jnp.zeros(halo.shape[1:], BF16)
-
-    @pl.when(has_high)
-    def _():
-        halo_down().wait_recv()
-
-    @pl.when(jnp.logical_not(has_high))
-    def _():
-        halo[1] = jnp.zeros(halo.shape[1:], BF16)
-
-    @pl.loop(0, dates // 16)
-    def _(g):
-        taps = taps_of(g)
-        for part in range(2):
-            at, row = fir_rows(part, g)
-            low = [halo[0, q, at, :].astype(F32) for q in range(reach)]
-            low += [row(q) for q in range(2 * reach)]
-            high = [row(rows - 2 * reach + q) for q in range(2 * reach)]
-            high += [halo[1, q, at, :].astype(F32) for q in range(reach)]
-            for i in range(reach):
-                fir(i, at, taps, low[i : i + taps_count])
-                fir(rows - reach + i, at, taps, high[i : i + taps_count])
-
-    def w_copy(o, src):
-        return remote(
-            wsend.at[peers[o]], what.at[src],
-            s_w.at[o], r_w.at[src], peers[o], az,
-        )
-
-    for o in list(range(1, groups)) + [0]:
-        b = peers[o]
-        if o:
-            idx_copy(o, b).wait_recv()
-        chosen = idx_all[b][0:1, :]
-        pixel = lax.broadcasted_iota(jnp.int32, (block_rows * cols, 2 * looks), 0)
-        pick = (pixel == chosen).astype(F32).astype(BF16)
-        sample = jnp.dot(z[b], pick, preferred_element_type=F32)
-        left = lax.broadcasted_iota(jnp.int32, (dates, 2 * looks), 1) < looks
-        sample = jnp.where(left, sample[:dates], sample[dates:]).astype(BF16)
-        if o:
-            wsend[b] = sample
-            w_copy(o, me).start()
-        else:
-            what[me] = sample
     for o in range(1, groups):
-        w_copy(o, peers[o]).wait_recv()
+        w_copy(peers[o], peers[o]).wait_recv()
 
     tops = []
     both = []
@@ -456,7 +470,7 @@
     for o in range(groups):
         if o:
             idx_copy(o, me).wait_send()
-            w_copy(o, me).wait_send()
+            w_copy(peers[o], me).wait_send()
             v_copy(o, me).wait_send()
             for chunk in range(3):
                 p_copy(o, me, chunk).wait_send()
@@ -482,6 +496,7 @@
     vmem = pl.BlockSpec(memory_space=pltpu.VMEM)
     scratch = [
         pltpu.VMEM((2 * dates * pitch, cols), F32),
+        pltpu.VMEM((taps_count, dates, cols), F32),
         pltpu.VMEM((2, taps_count // 2, 2 * dates, cols), BF16),
         pltpu.VMEM((2, taps_count // 2, 2 * dates, cols), BF16),
         pltpu.VMEM((8, 2 * looks), jnp.int32),
@@ -517,7 +532,7 @@
             collective_id=0, has_side_effects=True, vmem_limit_bytes=60 * 2**20
         ),
     )(
-        slc_stack, fir_taps, look_index.reshape(1, looks), shrink_level,
+        slc_stack, fir_taps.T, look_index.reshape(1, looks), shrink_level,
         window_half.reshape(1, all_dates), basis,
     )
     return out.reshape(own, 2, rows, cols)

time: 38.3 us -> 36.6 us (0.956)
  Pallas kernels: 35 us -> 34.1 us
  local copies, waits for them, and re-layouts: 2.4 us -> 1.67 us
    pallas_call x1, Pallas kernels: 35 us -> 34.1 us  [on_device(): pl.pallas_call(functools.partial(kernel, groups, slabs, unit, own, pitch)...]
    unnamed x4 -> x1, local copies, waits for them, and re-layouts: 2.4 us -> 1.67 us
where the time goes in v6:
time: 36.6 us; the launch traced here: 36.4 us
  Pallas kernels  34.1 us (93%)
  local copies, waits for them, and re-layouts  1.67 us (5%)
  between operations  0.66 us (2%)
    pallas_call x1, Pallas kernels, on_device(): pl.pallas_call(functools.partial(kernel, groups, slabs, unit, own, pitch)...  34.1 us
    unnamed x1, local copies, waits for them, and re-layouts  1.67 us

profile of v6, /device:TPU:0, one launch (start us, length us, event | category | flops | bytes accessed | tf_op | source)
XLA Modules:
  0.0 36.4 jit_solution(11061420850922413198)
XLA Ops:
  0.7 34.1 %shard_map.64 = f32[512,128]{1,0:T(8,128)} custom-call(bf16[2,64,32,128]{3,2,1,0:T(8,128)(2,1)} %x_ref.1, f32[5,64]{1,0:T(8,128)} %bitcast.5, s32[1,64]{1,0:T(1,128)} %bitcast.7, s32[1,1]{1,0:T(1,128)S(6)} %copy.8.level_ref, s32[1,256]{1,0:T(1,128)} %bitcast.6, bf16[32,256]{1,0:T(8,128)(2,1)} %basis_ref.1), custom_call_target="tpu_custom_call" | custom-call | tf_op jit(solution)/shard_map/pallas_call | solution.py:525
  34.8 1.7 %copy.9 = f32[8,2,32,128]{3,2,1,0:T(8,128)} copy(f32[8,2,32,128]{3,2,1,0:T(8,128)} %bitcast.4) | data formatting | bytes 524288

commit v7 on v6

--- a/solution.py
+++ b/solution.py
@@ -114,8 +114,8 @@
     groups, slabs, unit, own, pitch,
     x_ref, taps_ref, look_ref, level_ref, window_ref, basis_ref, out_ref,
     xf, taps_wide, halo_send, halo, idx_send, idx_all, masked_ref, spread_ref, order_ref,
-    z, wsend, what, vsend, vrecv, u, mine, psend, precv, esend, erecv,
-    s_halo, r_halo, s_idx, r_idx, s_w, r_w, s_v, r_v, s_p, r_p, s_e, r_e,
+    z, wsend, what, vsend, vrecv, u, mine, psend, precv, relay, esend, erecv,
+    s_halo, r_halo, s_idx, r_idx, s_w, r_w, s_v, r_v, s_p, r_p, r_r, s_e, r_e,
 ):
     me = lax.axis_index("date")
     az = lax.axis_index("az")
@@ -416,13 +416,44 @@
 
         smooth_block(side * (groups - 1), d, put_edge)
 
-    for o in range(1, groups):
+    relayed = groups == 4
+    at_end = (me == 0) | (me == groups - 1)
+    is_far = {1: me == groups - 1, groups - 1: me == 0} if relayed else {}
+
+    def relay_copy(o, chunk):
+        return remote(
+            psend.at[peers[o], chunks[chunk]], relay.at[chunks[chunk]],
+            s_p.at[chunk, o], r_r.at[chunk], jnp.where(me == 0, 1, groups - 2), az,
+        )
+
+    def send_part(o, chunk):
+        if o in is_far:
+            pl.when(is_far[o])(lambda: relay_copy(o, chunk).start())
+            pl.when(jnp.logical_not(is_far[o]))(lambda: p_copy(o, me, chunk).start())
+        else:
+            p_copy(o, me, chunk).start()
+
+    def put_relayed(d):
+        def put(r, row):
+            psend[d, r] = (row + relay[r].astype(F32)).astype(BF16)
+
+        return put
+
+    direct = list(is_far) if relayed else list(range(1, groups))
+    if relayed:
+
+        @pl.when(at_end)
+        def _():
+            relay[...] = jnp.zeros(relay.shape, BF16)
+            precv[groups - 1 - me] = jnp.zeros(precv.shape[1:], BF16)
+
+    for o in direct:
 
         @pl.loop(1, groups - 1)
         def _(b, o=o):
             smooth_block(b, peers[o], put_sent(peers[o]))
 
-        p_copy(o, me, 0).start()
+        send_part(o, 0)
 
     @pl.when(has_low)
     def _():
@@ -440,10 +471,28 @@
     def _():
         erecv[1] = jnp.zeros(erecv.shape[1:], BF16)
 
-    for o in range(1, groups):
+    for o in direct:
         for side in range(2):
             edge_block(side, peers[o], put_sent(peers[o]))
-            p_copy(o, me, 1 + side).start()
+            send_part(o, 1 + side)
+
+    if relayed:
+        last = peers[2]
+        for chunk in range(3):
+
+            @pl.when(jnp.logical_not(at_end))
+            def _(chunk=chunk):
+                relay_copy(2, chunk).wait_recv()
+
+            if chunk == 0:
+
+                @pl.loop(1, groups - 1)
+                def _(b):
+                    smooth_block(b, last, put_relayed(last))
+
+            else:
+                edge_block(chunk - 1, last, put_relayed(last))
+            send_part(2, chunk)
 
     @pl.loop(1, groups - 1)
     def _(b):
@@ -454,7 +503,14 @@
 
     for chunk in range(3):
         for o in range(1, groups):
-            p_copy(o, peers[o], chunk).wait_recv()
+            if o in is_far:
+
+                @pl.when(jnp.logical_not(is_far[o]))
+                def _(o=o, chunk=chunk):
+                    p_copy(o, peers[o], chunk).wait_recv()
+
+            else:
+                p_copy(o, peers[o], chunk).wait_recv()
 
     @pl.loop(0, groups)
     def _(b):
@@ -513,13 +569,14 @@
         pltpu.VMEM((rows, unit, cols), F32),
         pltpu.VMEM((groups, rows, unit, cols), BF16),
         pltpu.VMEM((groups, rows, unit, cols), BF16),
+        pltpu.VMEM((rows, unit, cols), BF16),
         pltpu.VMEM((2, SMOOTH_REACH, groups, unit, cols), BF16),
         pltpu.VMEM((2, SMOOTH_REACH, groups, unit, cols), BF16),
         dma((2,)), dma((2,)),
         dma((groups,)), dma((groups,)),
         dma((groups,)), dma((groups,)),
         dma((groups,)), dma((groups,)),
-        dma((3, groups)), dma((3, groups)),
+        dma((3, groups)), dma((3, groups)), dma((3,)),
         dma((2,)), dma((2,)),
     ]
     out = pl.pallas_call(

time: 36.6 us -> 37.9 us (1.036)
  Pallas kernels: 34.1 us -> 35.4 us
    pallas_call x1, Pallas kernels: 34.1 us -> 35.4 us  [on_device(): pl.pallas_call(functools.partial(kernel, groups, slabs, unit, own, pitch)...]
where the time goes in v7:
time: 37.9 us; the launch traced here: 37.7 us
  Pallas kernels  35.4 us (93%)
  local copies, waits for them, and re-layouts  1.67 us (4%)
  between operations  0.66 us (2%)
    pallas_call x1, Pallas kernels, on_device(): pl.pallas_call(functools.partial(kernel, groups, slabs, unit, own, pitch)...  35.4 us
    unnamed x1, local copies, waits for them, and re-layouts  1.67 us

profile of v7, /device:TPU:0, one launch (start us, length us, event | category | flops | bytes accessed | tf_op | source)
XLA Modules:
  0.0 37.7 jit_solution(2095270364620866335)
XLA Ops:
  0.7 35.4 %shard_map.64 = f32[512,128]{1,0:T(8,128)} custom-call(bf16[2,64,32,128]{3,2,1,0:T(8,128)(2,1)} %x_ref.1, f32[5,64]{1,0:T(8,128)} %bitcast.5, s32[1,64]{1,0:T(1,128)} %bitcast.7, s32[1,1]{1,0:T(1,128)S(6)} %copy.8.level_ref, s32[1,256]{1,0:T(1,128)} %bitcast.6, bf16[32,256]{1,0:T(8,128)(2,1)} %basis_ref.1), custom_call_target="tpu_custom_call" | custom-call | tf_op jit(solution)/shard_map/pallas_call | solution.py:582
  36.0 1.7 %copy.9 = f32[8,2,32,128]{3,2,1,0:T(8,128)} copy(f32[8,2,32,128]{3,2,1,0:T(8,128)} %bitcast.4) | data formatting | bytes 524288

commit v8 on v6

--- a/solution.py
+++ b/solution.py
@@ -416,7 +416,8 @@
 
         smooth_block(side * (groups - 1), d, put_edge)
 
-    for o in range(1, groups):
+    far_first = sorted(range(1, groups), key=lambda o: abs(o - groups // 2))
+    for o in far_first:
 
         @pl.loop(1, groups - 1)
         def _(b, o=o):
@@ -440,7 +441,7 @@
     def _():
         erecv[1] = jnp.zeros(erecv.shape[1:], BF16)
 
-    for o in range(1, groups):
+    for o in far_first:
         for side in range(2):
             edge_block(side, peers[o], put_sent(peers[o]))
             p_copy(o, me, 1 + side).start()

time: 36.6 us -> 36.6 us (level)
  no operation moved by 1% of the time
where the time goes in v8:
time: 36.6 us; the launch traced here: 36.5 us
  Pallas kernels  34.1 us (93%)
  local copies, waits for them, and re-layouts  1.67 us (5%)
  between operations  0.66 us (2%)
    pallas_call x1, Pallas kernels, on_device(): pl.pallas_call(functools.partial(kernel, groups, slabs, unit, own, pitch)...  34.1 us
    unnamed x1, local copies, waits for them, and re-layouts  1.67 us

profile of v8, /device:TPU:0, one launch (start us, length us, event | category | flops | bytes accessed | tf_op | source)
XLA Modules:
  0.0 36.5 jit_solution(2934617556643720183)
XLA Ops:
  0.7 34.1 %shard_map.64 = f32[512,128]{1,0:T(8,128)} custom-call(bf16[2,64,32,128]{3,2,1,0:T(8,128)(2,1)} %x_ref.1, f32[5,64]{1,0:T(8,128)} %bitcast.5, s32[1,64]{1,0:T(1,128)} %bitcast.7, s32[1,1]{1,0:T(1,128)S(6)} %copy.8.level_ref, s32[1,256]{1,0:T(1,128)} %bitcast.6, bf16[32,256]{1,0:T(8,128)(2,1)} %basis_ref.1), custom_call_target="tpu_custom_call" | custom-call | tf_op jit(solution)/shard_map/pallas_call | solution.py:526
  34.8 1.7 %copy.9 = f32[8,2,32,128]{3,2,1,0:T(8,128)} copy(f32[8,2,32,128]{3,2,1,0:T(8,128)} %bitcast.4) | data formatting | bytes 524288
